TPU v7x, 512 devices: a whole 4x8x8 slice. The times are simulated.
512 devices in a mesh: gx: 32 (over z, x), gy: 16 (over y, core).
Axes of the slice: x: 4, y: 8, z: 8, core: 2. Of those that a mesh axis runs over, the one named last changes fastest.
Arguments:
- field: float32 [512, 256, 128], P('gx', 'gy'), may hold values from -6 to 6
- conductance: float32 [512, 256, 128], P('gx', 'gy'), may hold values from 200 to 5000
- source: float32 [512, 256, 128], P('gx', 'gy'), may hold values from -600 to 600
Outputs:
- advanced: float32 [512, 256, 128], P('gx', 'gy')
All inputs are finite; a program needn't handle non-finite values.
Results may differ from a plain program's by a relative error of at most 0.0003.
Values sent between devices are 32-bit elements; how exact they have to be, the bound alone decides.
No kernel may reach another device: no remote copies, remote signals or barrier semaphores. Data moves between devices by JAX's collectives and lax.ppermute only.
A program may use at most 64 MiB of HBM per device.

v0:
```python
import jax
import jax.numpy as jnp
from jax import lax
from jax.sharding import PartitionSpec as P


def with_halo(value, sides, width):
    edges = {}
    for axis, dim in sides:
        size, length = (lax.axis_size(axis), value.shape[dim])
        up = [(i, (i + 1) % size) for i in range(size - 1)]
        last = lax.slice_in_dim(value, length - width, length, axis=dim)
        first = lax.slice_in_dim(value, 0, width, axis=dim)
        edges[dim] = (
            lax.ppermute(last, axis, up),
            lax.ppermute(first, axis, [(b, a) for a, b in up]),
        )
    done = []
    for _, dim in sides:
        low, high = edges[dim]
        around = [(width, width) if d in done else (0, 0) for d in range(value.ndim)]
        value = jnp.concatenate([jnp.pad(low, around), value, jnp.pad(high, around)], axis=dim)
        done.append(dim)
    return value


def copy_for_each(value, axis):
    size = lax.axis_size(axis)
    return lax.all_to_all(
        jnp.broadcast_to(value[None], (size, *value.shape)), axis, 0, 0, tiled=True
    )


def all_in_one(value, axis):
    leaves = jax.tree.leaves(value)
    order = sorted(range(len(leaves)), key=lambda k: -leaves[k].size)
    width = (1, *leaves[order[0]].shape)[-1]
    lines = [
        jnp.pad(leaves[k].reshape(-1), (0, -leaves[k].size % width)).reshape(-1, width)
        for k in order
    ]
    both, at, found = (copy_for_each(jnp.concatenate(lines), axis), 0, {})
    for k, line in zip(order, lines):
        piece = both[:, at : at + len(line)].reshape(len(both), -1)
        found[k] = piece[:, : leaves[k].size].reshape(-1, *leaves[k].shape)
        at += len(line)
    numbers = iter(range(len(leaves)))
    return jax.tree.map(lambda _: found[next(numbers)], value)


def joined_by_halves(pieces, combine):
    while len(jax.tree.leaves(pieces)[0]) > 1:
        pieces = jax.vmap(combine)(
            *(jax.tree.map(lambda part: part[side::2], pieces) for side in (0, 1))
        )
    return jax.tree.map(lambda part: part[0], pieces)


def carried_in(value, axis, combine, identity, reverse):
    size, index = (lax.axis_size(axis), lax.axis_index(axis))
    passed = jnp.arange(size) > index if reverse else jnp.arange(size) < index

    def carried_kept(part, zero, own):
        part = jnp.where(
            passed.reshape(-1, *(1 for _ in own.shape)), part, jnp.asarray(zero, own.dtype)
        )
        return part[::-1] if reverse else part

    pieces = all_in_one(value, axis)
    return joined_by_halves(jax.tree.map(carried_kept, pieces, identity, value), combine)


def gathered_by_type(value, axis):
    leaves, found = (jax.tree.leaves(value), {})
    for first, a in enumerate(leaves):
        if first not in found:
            alike = [k for k, b in enumerate(leaves) if b.dtype == a.dtype]
            got = (
                all_in_one([leaves[k] for k in alike], axis)
                if len(alike) > 1
                else [copy_for_each(a, axis)]
            )
            for k, b in zip(alike, got):
                found[k] = b
    numbers = iter(range(len(leaves)))
    return jax.tree.map(lambda _: found[next(numbers)], value)


def entering(value, axis, combine, identity, reverse):
    size, index = (lax.axis_size(axis), lax.axis_index(axis))
    passed = jnp.arange(size) > index if reverse else jnp.arange(size) < index

    def entering_kept(part, zero, own):
        part = jnp.where(
            passed.reshape(-1, *(1 for _ in own.shape)), part, jnp.asarray(zero, own.dtype)
        )
        return part[::-1] if reverse else part

    pieces = gathered_by_type(value, axis)
    return joined_by_halves(jax.tree.map(entering_kept, pieces, identity, value), combine)


def thomas(lower, diag, upper, rights):
    stacked = jnp.stack(rights, axis=1)

    def forward_step(carry, items):
        prev_ratio, prev_value = carry
        low, dia, upp, rig = items
        pivot = dia - low * prev_ratio
        inverse = 1.0 / pivot
        ratio = upp * inverse
        value = (rig - low[None] * prev_value) * inverse[None]
        return ((ratio, value), (ratio, value))

    start = (jnp.zeros_like(diag[0]), jnp.zeros_like(stacked[0]))
    unused, (ratios, values) = lax.scan(forward_step, start, (lower, diag, upper, stacked))

    def backward_step(following, items):
        ratio, value = items
        solved = value - ratio[None] * following
        return (solved, solved)

    unused_back, solved = lax.scan(
        backward_step, jnp.zeros_like(stacked[0]), (ratios, values), reverse=True
    )
    return [solved[:, j] for j in range(len(rights))]


def join(left, right):
    pfa, afa, bfa, pla, ala, bla = left
    pfb, afb, bfb, plb, alb, blb = right
    scale = 1.0 / (1.0 - bla * afb)
    mid_p = (pla + bla * pfb) * scale
    mid_a = ala * scale
    mid_b = bla * bfb * scale
    next_p = pfb + afb * mid_p
    next_a = afb * mid_a
    next_b = bfb + afb * mid_b
    return (
        pfa + bfa * next_p,
        afa + bfa * next_a,
        bfa * next_b,
        plb + alb * mid_p,
        alb * mid_a,
        blb + alb * mid_b,
    )


def join_back(earlier, later):
    return join(later, earlier)


def neutral(sample):
    zeros = jnp.zeros_like(sample)
    ones = jnp.ones_like(sample)
    return (zeros, zeros, ones, zeros, ones, zeros)


def partitioned(lower, diag, upper, right, couple):
    length = diag.shape[0]
    inner = right[1:-1]
    zeros = jnp.zeros_like(inner)
    from_first = zeros.at[0].set(-lower[1])
    from_last = zeros.at[-1].set(-upper[length - 2])
    base, first_part, last_part = thomas(
        lower[1:-1], diag[1:-1], upper[1:-1], [inner, from_first, from_last]
    )
    top_a = diag[0] + upper[0] * first_part[0]
    top_b = upper[0] * last_part[0]
    top_r = right[0] - upper[0] * base[0]
    bot_a = lower[length - 1] * first_part[-1]
    bot_b = diag[length - 1] + lower[length - 1] * last_part[-1]
    bot_r = right[length - 1] - lower[length - 1] * base[-1]
    inverse = 1.0 / (top_a * bot_b - top_b * bot_a)
    edge_lo = lower[0]
    edge_hi = upper[length - 1]
    coeffs = (
        (bot_b * top_r - top_b * bot_r) * inverse,
        -bot_b * edge_lo * inverse,
        top_b * edge_hi * inverse,
        (top_a * bot_r - bot_a * top_r) * inverse,
        bot_a * edge_lo * inverse,
        -top_a * edge_hi * inverse,
    )
    before, after = couple(coeffs)
    pfo, afo, bfo, plo, alo, blo = coeffs
    prev_p, prev_b = (before[3], before[5])
    next_p, next_a = (after[0], after[1])
    m_ff = 1.0 - afo * prev_b
    m_fl = -bfo * next_a
    m_lf = -alo * prev_b
    m_ll = 1.0 - blo * next_a
    r_f = pfo + afo * prev_p + bfo * next_p
    r_l = plo + alo * prev_p + blo * next_p
    inverse = 1.0 / (m_ff * m_ll - m_fl * m_lf)
    first_val = (m_ll * r_f - m_fl * r_l) * inverse
    last_val = (m_ff * r_l - m_lf * r_f) * inverse
    middle = base + first_part * first_val + last_part * last_val
    return jnp.concatenate([first_val[None], middle, last_val[None]], axis=0)


def body(field, conductance, source):
    stacked = jnp.stack([field, conductance])
    padded = with_halo(stacked, (("gx", 1), ("gy", 2)), 1)
    nearby = padded[0]
    cond = padded[1]
    faces_x = 0.5 * (cond[:-1, 1:-1] + cond[1:, 1:-1])
    faces_y = 0.5 * (cond[1:-1, :-1] + cond[1:-1, 1:])
    cond_z = jnp.pad(conductance, ((0, 0), (0, 0), (1, 1)))
    faces_z = 0.5 * (cond_z[..., :-1] + cond_z[..., 1:])
    flux_x = faces_x * (nearby[1:, 1:-1] - nearby[:-1, 1:-1])
    apply_x = flux_x[1:] - flux_x[:-1]
    flux_y = faces_y * (nearby[1:-1, 1:] - nearby[1:-1, :-1])
    apply_y = flux_y[:, 1:] - flux_y[:, :-1]
    field_z = jnp.pad(field, ((0, 0), (0, 0), (1, 1)))
    flux_z = faces_z * (field_z[..., 1:] - field_z[..., :-1])
    apply_z = flux_z[..., 1:] - flux_z[..., :-1]
    first = field + 0.5 * apply_x + apply_y + apply_z + source

    def couple_x(coeffs):
        start = neutral(coeffs[0])
        before = carried_in(coeffs, "gx", join, start, False)
        after = carried_in(coeffs, "gx", join_back, start, True)
        return (before, after)

    def couple_y(coeffs):
        start = neutral(coeffs[0])
        before = entering(coeffs, "gy", join, start, False)
        after = entering(coeffs, "gy", join_back, start, True)
        return (before, after)

    lower_x = -0.5 * faces_x[:-1]
    upper_x = -0.5 * faces_x[1:]
    section_x = partitioned(lower_x, 1.0 - lower_x - upper_x, upper_x, first, couple_x)
    moved_faces = jnp.moveaxis(faces_y, 1, 0)
    lower_y = -0.5 * moved_faces[:-1]
    upper_y = -0.5 * moved_faces[1:]
    second = jnp.moveaxis(section_x - 0.5 * apply_y, 1, 0)
    section_y = jnp.moveaxis(
        partitioned(lower_y, 1.0 - lower_y - upper_y, upper_y, second, couple_y), 0, 1
    )
    rows_x, rows_y, depth = field.shape
    third = jnp.moveaxis(section_y - 0.5 * apply_z, 2, 0).reshape(depth, rows_x * rows_y)
    flat_faces = jnp.moveaxis(faces_z, 2, 0).reshape(depth + 1, rows_x * rows_y)
    lower_z = -0.5 * flat_faces[:-1]
    upper_z = -0.5 * flat_faces[1:]
    solved = thomas(lower_z, 1.0 - lower_z - upper_z, upper_z, [third])[0]
    return jnp.moveaxis(solved.reshape(depth, rows_x, rows_y), 0, 2)


def solution(mesh):
    return jax.shard_map(
        body,
        mesh=mesh,
        in_specs=(P("gx", "gy", None), P("gx", "gy", None), P("gx", "gy", None)),
        out_specs=P("gx", "gy", None),
        check_vma=False,
    )
```

profile of v0, /device:TPU:1, one launch (start us, length us, event | category | flops | bytes accessed | tf_op | source)
XLA Modules:
  0.0 146.0 jit_solution(10239100589400499075)
XLA Ops:
  0.0 1.1 copy_bitcast_fusion
  1.1 4.6 %collective-permute-start = (f32[2,16,1,128]{3,1,2,0:T(8,128)S(1)}, f32[2,16,1,128]{3,1,2,0:T(8,128)S(1)}, u32[]{:S(2)}, u32[]{:S(2)}) collective-permute-start(f32[2,16,1,128]{3,1,2,0:T(8,128)S(1)} %get-tuple-element.935), channel_id=1, source_target_pairs={{0,1},{1,2},{2,3},{3,4},{4,5},{5,6},{6,7},{7,8},{8,9},{9,10},{10,1... | collective-permute-start | bytes 49160 | tf_op jit(solution)/shard_map/ppermute | solution.py:15
  5.7 3.1 %collective-permute-start.1 = (f32[2,1,16,128]{3,1,2,0:T(1,128)S(1)}, f32[2,1,16,128]{3,1,2,0:T(1,128)S(1)}, u32[]{:S(2)}, u32[]{:S(2)}) collective-permute-start(f32[2,1,16,128]{3,1,2,0:T(1,128)S(1)} %get-tuple-element.933), channel_id=1, source_target_pairs={{0,16},{16,32},{32,48},{48,64},{64,80},{80,96},{96,112},{112,128},... | collective-permute-start | bytes 49160 | tf_op jit(solution)/shard_map/ppermute | solution.py:15
  8.8 1.3 collective-permute-start.2
  10.1 3.7 %collective-permute-start.3 = (f32[2,16,1,128]{3,1,2,0:T(8,128)S(1)}, f32[2,16,1,128]{3,1,2,0:T(8,128)S(1)}, u32[]{:S(2)}, u32[]{:S(2)}) collective-permute-start(f32[2,16,1,128]{3,1,2,0:T(8,128)S(1)} %get-tuple-element.936), channel_id=1, source_target_pairs={{1,0},{2,1},{3,2},{4,3},{5,4},{6,5},{7,6},{8,7},{9,8},{10,9},{11,1... | collective-permute-start | bytes 49160 | tf_op jit(solution)/shard_map/ppermute | solution.py:16
  14.1 1.1 collective-permute-done.3
  16.6 0.9 while.106
  17.5 0.8 while.107
  18.5 1.3 broadcast_in_dim.215
  19.8 14.6 %all-to-all-start = ((f32[32,96,128]{2,1,0:T(8,128)}), f32[32,96,128]{2,1,0:T(8,128)S(1)}, u32[]{:S(2)}, u32[]{:S(2)}) async-start(f32[32,96,128]{2,1,0:T(8,128)} %broadcast_in_dim.215), calls=%async_computation | async-start | bytes 3145728 | tf_op jit(solution)/shard_map/all_to_all | solution.py:29
  38.3 1.3 subtract_divide_fusion.21
  39.7 33.0 %all-to-all-done = f32[32,96,128]{2,1,0:T(8,128)S(1)} async-done(((f32[32,96,128]{2,1,0:T(8,128)}), f32[32,96,128]{2,1,0:T(8,128)S(1)}, u32[]{:S(2)}, u32[]{:S(2)}) %all-to-all-start) | async-done | bytes 1572896 | tf_op jit(solution)/shard_map/all_to_all | solution.py:29
  72.7 1.0 slice_select_fusion.6
  75.2 0.8 subtract_multiply_fusion.3
  76.2 10.9 %while.108 = (s32[]{:T(128)}, f32[16,128]{1,0:T(8,128)S(1)}, f32[3,16,128]{2,1,0:T(8,128)S(1)}, f32[14,16,128]{2,1,0:T(8,128)S(1)}, f32[14,3,16,128]{3,2,1,0:T(8...) while((s32[]{:T(128)}, f32[16,128]{1,0:T(8,128)S(1)}, ...), condition=%wide.region_5.6_spmd.clone, body=%wide.region_4.5_spmd.clone.sunk | while | flops 34819 | bytes 180352 | solution.py:116
  76.2 0.7 bitcast_dynamic-update-slice_fusion.17
  77.0 0.7 bitcast_dynamic-update-slice_fusion.17
  77.7 0.7 bitcast_dynamic-update-slice_fusion.17
  78.5 0.7 bitcast_dynamic-update-slice_fusion.17
  79.3 0.7 bitcast_dynamic-update-slice_fusion.17
  80.1 0.7 bitcast_dynamic-update-slice_fusion.17
  80.9 0.7 bitcast_dynamic-update-slice_fusion.17
  81.6 0.7 bitcast_dynamic-update-slice_fusion.17
  83.2 0.7 bitcast_dynamic-update-slice_fusion.17
  85.5 0.7 bitcast_dynamic-update-slice_fusion.17
  87.1 0.8 while.109
  88.7 1.0 broadcast_in_dim.220
  89.7 8.0 %all-to-all-start.1 = ((f32[16,96,128]{2,1,0:T(8,128)}), f32[16,96,128]{2,1,0:T(8,128)S(1)}, u32[]{:S(2)}, u32[]{:S(2)}) async-start(f32[16,96,128]{2,1,0:T(8,128)} %broadcast_in_dim.220), calls=%async_computation.1 | async-start | bytes 1572864 | tf_op jit(solution)/shard_map/all_to_all | solution.py:29
  99.0 21.3 %all-to-all-done.1 = f32[16,96,128]{2,1,0:T(8,128)S(1)} async-done(((f32[16,96,128]{2,1,0:T(8,128)}), f32[16,96,128]{2,1,0:T(8,128)S(1)}, u32[]{:S(2)}, u32[]{:S(2)}) %all-to-all-start.1) | async-done | bytes 786464 | tf_op jit(solution)/shard_map/all_to_all | solution.py:29
  121.6 18.7 %while.110 = (s32[]{:T(128)}, f32[256]{0:T(256)S(1)}, f32[1,256]{1,0:T(1,128)S(1)}, f32[128,256]{1,0:T(8,128)S(1)}, f32[128,1,256]{2,1,0:T(1,128)S(1)}, /*index=...) while((s32[]{:T(128)}, f32[256]{0:T(256)S(1)}, ...), condition=%wide.region_9.10_spmd.clone, body=%wide.region_8.9_spmd.clone.sunk | while | flops 2307 | bytes 20616 | solution.py:116
  140.3 4.8 %while.111 = (s32[]{:T(128)}, f32[1,256]{1,0:T(1,128)S(1)}, f32[128,1,256]{2,1,0:T(1,128)S(1)}, f32[128,1,256]{2,1,0:T(1,128)S(1)}, f32[128,256]{1,0:T(8,128)S(1)}, /*index=5*/s32[]{:T(128)}, s32[]{:T(128)}, s32[]{:T(128)}) while((s32[]{:T(128)}, f32[1,256]{1,0:T(1,128)S(1)}, f32[128,1,256]{2,1,0:T(1,128)S(1)}, ...), condition=%wide.region_11.12_spmd.clone, body=%wide.region_10.11_spmd.clone.sunk | while | flops 772 | bytes 5231 | solution.py:123
  145.2 0.8 copy.103
  (1027 shorter events, 29.7 us)
Async XLA Ops:
  1.1 13.0 %collective-permute-start = (f32[2,16,1,128]{3,1,2,0:T(8,128)S(1)}, f32[2,16,1,128]{3,1,2,0:T(8,128)S(1)}, u32[]{:S(2)}, u32[]{:S(2)}) collective-permute-start(f32[2,16,1,128]{3,1,2,0:T(8,128)S(1)} %get-tuple-element.935), channel_id=1, source_target_pairs={{0,1},{1,2},{2,3},{3,4},{4,5},{5,6},{6,7},{7,8},{8,9},{9,10},{10,1... | collective-permute-start | bytes 49160 | tf_op jit(solution)/shard_map/ppermute | solution.py:15
  5.7 8.4 %collective-permute-start.1 = (f32[2,1,16,128]{3,1,2,0:T(1,128)S(1)}, f32[2,1,16,128]{3,1,2,0:T(1,128)S(1)}, u32[]{:S(2)}, u32[]{:S(2)}) collective-permute-start(f32[2,1,16,128]{3,1,2,0:T(1,128)S(1)} %get-tuple-element.933), channel_id=1, source_target_pairs={{0,16},{16,32},{32,48},{48,64},{64,80},{80,96},{96,112},{112,128},... | collective-permute-start | bytes 49160 | tf_op jit(solution)/shard_map/ppermute | solution.py:15
  8.8 5.3 %collective-permute-start.2 = (f32[2,1,16,128]{3,1,2,0:T(1,128)S(1)}, f32[2,1,16,128]{3,1,2,0:T(1,128)S(1)}, u32[]{:S(2)}, u32[]{:S(2)}) collective-permute-start(f32[2,1,16,128]{3,1,2,0:T(1,128)S(1)} %get-tuple-element.934), channel_id=1, source_target_pairs={{16,0},{32,16},{48,32},{64,48},{80,64},{96,80},{112,96},{128,112},... | collective-permute-start | bytes 49160 | tf_op jit(solution)/shard_map/ppermute | solution.py:16
  10.1 5.1 %collective-permute-start.3 = (f32[2,16,1,128]{3,1,2,0:T(8,128)S(1)}, f32[2,16,1,128]{3,1,2,0:T(8,128)S(1)}, u32[]{:S(2)}, u32[]{:S(2)}) collective-permute-start(f32[2,16,1,128]{3,1,2,0:T(8,128)S(1)} %get-tuple-element.936), channel_id=1, source_target_pairs={{1,0},{2,1},{3,2},{4,3},{5,4},{6,5},{7,6},{8,7},{9,8},{10,9},{11,1... | collective-permute-start | bytes 49160 | tf_op jit(solution)/shard_map/ppermute | solution.py:16
  15.3 0.9 copy-start.3
  15.3 1.0 copy-start.5
  15.6 2.8 %copy-start.2 = (f32[16,16,128]{2,1,0:T(8,128)}, f32[16,16,128]{2,1,0:T(8,128)S(1)}, u32[]{:S(2)}) copy-start(f32[16,16,128]{2,1,0:T(8,128)S(1)} %get-tuple-element.985) | copy-start | bytes 393220
  15.6 2.9 %copy-start = (f32[16,16,128]{2,1,0:T(8,128)}, f32[16,16,128]{2,1,0:T(8,128)S(1)}, u32[]{:S(2)}) copy-start(f32[16,16,128]{2,1,0:T(8,128)S(1)} %get-tuple-element.986) | copy-start | bytes 393220
  16.4 2.0 %copy-start.6 = (f32[1,16,128]{2,0,1:T(1,128)}, f32[1,16,128]{2,0,1:T(1,128)S(1)}, u32[]{:S(2)}) copy-start(f32[1,16,128]{2,0,1:T(1,128)S(1)} %get-tuple-element.982) | copy-start | bytes 24580
  16.4 2.0 %copy-start.8 = (f32[1,16,128]{2,0,1:T(1,128)}, f32[1,16,128]{2,0,1:T(1,128)S(1)}, u32[]{:S(2)}) copy-start(f32[1,16,128]{2,0,1:T(1,128)S(1)} %get-tuple-element.983) | copy-start | bytes 24580
  19.8 52.9 %all-to-all-start = ((f32[32,96,128]{2,1,0:T(8,128)}), f32[32,96,128]{2,1,0:T(8,128)S(1)}, u32[]{:S(2)}, u32[]{:S(2)}) async-start(f32[32,96,128]{2,1,0:T(8,128)} %broadcast_in_dim.215), calls=%async_computation | async-start | bytes 3145728 | tf_op jit(solution)/shard_map/all_to_all | solution.py:29
  35.2 3.2 %copy-start.1 = (f32[16,16,128]{2,1,0:T(8,128)}, f32[16,16,128]{2,1,0:T(8,128)S(1)}, u32[]{:S(2)}) copy-start(f32[16,16,128]{2,1,0:T(8,128)S(1)} %get-tuple-element.963) | copy-start | bytes 393220
  74.4 0.7 copy-start.7
  74.4 0.7 copy-start.9
  74.4 0.7 copy-start.10
  74.4 0.7 copy-start.11
  74.4 0.7 copy-start.12
  74.6 1.5 %copy-start.13 = (f32[1,1,16,128]{3,2,1,0:T(8,128)S(1)}, f32[1,1,16,128]{3,2,1,0:T(8,128)}, u32[]{:S(2)}) copy-start(f32[1,1,16,128]{3,2,1,0:T(8,128)} %fusion.63) | copy-start | bytes 24580
  74.6 1.5 %copy-start.14 = (f32[1,1,16,128]{3,2,1,0:T(8,128)S(1)}, f32[1,1,16,128]{3,2,1,0:T(8,128)}, u32[]{:S(2)}) copy-start(f32[1,1,16,128]{3,2,1,0:T(8,128)} %fusion.64) | copy-start | bytes 24580
  74.7 1.5 %copy-start.4 = (f32[16,128]{1,0:T(8,128)S(1)}, f32[16,128]{1,0:T(8,128)}, u32[]{:S(2)}) copy-start(f32[16,128]{1,0:T(8,128)} %custom-call.3) | copy-start | bytes 24580
  89.7 30.6 %all-to-all-start.1 = ((f32[16,96,128]{2,1,0:T(8,128)}), f32[16,96,128]{2,1,0:T(8,128)S(1)}, u32[]{:S(2)}, u32[]{:S(2)}) async-start(f32[16,96,128]{2,1,0:T(8,128)} %broadcast_in_dim.220), calls=%async_computation.1 | async-start | bytes 1572864 | tf_op jit(solution)/shard_map/all_to_all | solution.py:29
where the time goes:
time: 148 us; the launch traced here: 146 us
  waiting for transfers between devices  55.4 us (37%)
  starting transfers between devices  35.2 us (24%)
  other arithmetic  27.3 us (18%)
  local copies, waits for them, and re-layouts  17.1 us (12%)
  loops' own time  9.8 us (7%)
    all_to_all x2, waiting for transfers between devices, copy_for_each(): lax.all_to_all(jnp.broadcast_to(value[None], (size, *value.shape)), axis,...  54.4 us
    all_to_all x2, starting transfers between devices, copy_for_each(): lax.all_to_all(jnp.broadcast_to(value[None], (size, *value.shape)), axis,...  22.6 us
    dynamic_update_slice x340, other arithmetic, thomas(): lax.scan(forward_step, start, (lower, diag, upper, stacked))  16.5 us
    ppermute x2, starting transfers between devices, with_halo(): lax.ppermute(last, axis, up)  7.71 us
    another operation x3, loops' own time, thomas(): lax.scan(forward_step, start, (lower, diag, upper, stacked))  6.46 us
    dynamic_update_slice x128, local copies, waits for them, and re-layouts, thomas(): lax.scan(forward_step, start, (lower, diag, upper, stacked))  5.52 us
    ppermute x2, starting transfers between devices, with_halo(): lax.ppermute(first, axis, [(b, a) for a, b in up])  4.95 us
    another operation x3, loops' own time, thomas(): lax.scan(backward_step, jnp.zeros_like(stacked[0]), (ratios, values), rev...  3.34 us
  transfers between devices with their start and end apart: 6, of which 3 were waited for; matrix products, arithmetic and copies ran while one was open for 5% of the time, Pallas kernels for 0%

commit v1 on v0

v1 whole, which is shorter than its diff:
```python
import jax
import jax.numpy as jnp
from jax import lax
from jax.experimental import pallas as pl
from jax.experimental.pallas import tpu as pltpu
from jax.sharding import PartitionSpec as P

N = 16
LANES = 128
ROUNDS = (1, 2, 4, 8, 16, 32, 64)
VALUES = 8


def rows(k):
    return pl.ds(N * k, N)


def turned(k):
    return pl.ds(k, N, stride=N)


def shape(*dims):
    return jax.ShapeDtypeStruct(dims, jnp.float32)


def eliminated(cells, emit):
    one = jnp.ones_like(cells[0])
    half = [None] + [0.25 * (cells[k - 1] + cells[k]) for k in range(1, N)]
    first, excess, excess_first = half[1], one, one
    for k in range(1, N - 1):
        g = 1.0 / (first + half[k + 1] + excess)
        n = first * g
        m = half[k + 1] * g
        emit(k, g, n, m)
        excess_first = excess_first + n * excess
        first = m * first
        excess = one + m * excess
    return first, excess_first, excess


def prepare_kernel(f_ref, c_ref, s_ref, rhs_ref, g_ref, n_ref, m_ref, mat_ref, ay_ref):
    def emit(k, g, n, m):
        g_ref[rows(k), :] = g
        n_ref[rows(k), :] = n
        m_ref[rows(k + 1), :] = m

    cells = [c_ref[rows(k), :] for k in range(N)]
    q, e0, e1 = eliminated(cells, emit)
    for k, part in enumerate((q, e0, e1)):
        mat_ref[rows(k), :] = part
    flux = None
    for y in range(N - 1):
        c0, c1 = c_ref[turned(y), :], c_ref[turned(y + 1), :]
        f0, f1 = f_ref[turned(y), :], f_ref[turned(y + 1), :]
        after = 0.5 * (c0 + c1) * (f1 - f0)
        ay_ref[turned(y), :] = after if flux is None else after - flux
        flux = after
    ay_ref[turned(N - 1), :] = -flux
    lane = lax.broadcasted_iota(jnp.int32, (N, LANES), 1)
    for k in range(N):
        c, f = cells[k], f_ref[rows(k), :]
        c_next = jnp.where(lane < LANES - 1, pltpu.roll(c, LANES - 1, 1), 0.0)
        f_next = jnp.where(lane < LANES - 1, pltpu.roll(f, LANES - 1, 1), 0.0)
        upper = 0.5 * (c + c_next) * (f_next - f)
        lower = jnp.where(lane > 0, pltpu.roll(upper, 1, 1), 0.5 * c * f)
        rhs_ref[rows(k), :] = 2.0 * f + s_ref[rows(k), :] + ay_ref[rows(k), :] + (upper - lower)


def x_forward_kernel(
    f_ref, c_ref, rhs_ref, g_ref, n_ref, m_ref, mat_ref, down_ref, up_ref, gr_ref, pay_ref, r_ref
):
    r_ref[...] = rhs_ref[...]
    flux_down = 0.5 * (down_ref[rows(1), :] + c_ref[turned(0), :]) * (
        f_ref[turned(0), :] - down_ref[rows(0), :]
    )
    flux_up = 0.5 * (up_ref[rows(1), :] + c_ref[turned(N - 1), :]) * (
        up_ref[rows(0), :] - f_ref[turned(N - 1), :]
    )
    r_ref[turned(0), :] = r_ref[turned(0), :] - flux_down
    r_ref[turned(N - 1), :] = r_ref[turned(N - 1), :] + flux_up
    r0, r1 = forward(lambda k: r_ref[rows(k), :], g_ref, n_ref, m_ref, gr_ref)
    values = [mat_ref[rows(k), :] for k in range(3)]
    values += [c_ref[rows(0), :], c_ref[rows(N - 1), :], r0, r1, jnp.zeros_like(r0)]
    for k, value in enumerate(values):
        pay_ref[pl.ds(k, N, stride=VALUES), :] = value
        pay_ref[pl.ds(N * VALUES + k, N, stride=VALUES), :] = value


def forward(right, g_ref, n_ref, m_ref, gr_ref):
    r0, carried = right(0), None
    for k in range(1, N):
        carried = right(k) if carried is None else right(k) + m_ref[rows(k), :] * carried
        if k < N - 1:
            r0 = r0 + n_ref[rows(k), :] * carried
            gr_ref[rows(k), :] = g_ref[rows(k), :] * carried
    return r0, carried


def backward(u0, u1, gr_ref, n_ref, m_ref, emit):
    emit(0, u0)
    emit(N - 1, u1)
    later = u1
    for k in range(N - 2, 0, -1):
        later = gr_ref[rows(k), :] + n_ref[rows(k), :] * u0 + m_ref[rows(k + 1), :] * later
        emit(k, later)


def coupled(in_ref, blocks):
    q, e0, e1, c0, c1, r0, r1 = (
        in_ref[pl.ds(k, blocks, stride=VALUES), :] for k in range(VALUES - 1)
    )
    block = lax.broadcasted_iota(jnp.int32, (blocks, LANES), 0)

    def before(value, s=1):
        return pltpu.roll(value, s, 0)

    def after(value, s=1):
        return pltpu.roll(value, blocks - s, 0)

    inside_low = block > 0
    inside_high = block < blocks - 1
    low = 0.25 * (jnp.where(inside_low, before(c1), 0.0) + c0)
    high = 0.25 * (jnp.where(inside_high, after(c0), 0.0) + c1)
    e0 = e0 + jnp.where(inside_low, 0.0, low)
    e1 = e1 + jnp.where(inside_high, 0.0, high)
    low = jnp.where(inside_low, low, 0.0)
    high = jnp.where(inside_high, high, 0.0)
    h = 1.0 / (q + high + e1)
    qh, eh, rh = q * h, e1 * h, r1 * h
    lower = low * before(qh)
    upper = qh * high
    excess = e0 + q * eh + low * before(eh)
    right = r0 + q * rh + low * before(rh)
    s = 1
    while s < blocks:
        g = 1.0 / (lower + upper + excess)
        lg, ug, eg, rg = lower * g, upper * g, excess * g, right * g
        excess = excess + lower * before(eg, s) + upper * after(eg, s)
        right = right + lower * before(rg, s) + upper * after(rg, s)
        lower, upper = lower * before(lg, s), upper * after(ug, s)
        s *= 2
    u0 = right / excess
    u1 = rh + qh * u0 + (high * h) * after(u0)
    return u0, u1


def x_middle_kernel(blocks, in_ref, out_ref):
    u0, u1 = coupled(in_ref, blocks)
    out_ref[...] = jnp.where(lax.axis_index("gx") < N, u0, u1)


def y_middle_kernel(blocks, in_ref, out_ref):
    u0, u1 = coupled(in_ref, blocks)
    out_ref[pl.ds(0, blocks, stride=2), :] = u0
    out_ref[pl.ds(1, blocks, stride=2), :] = u1


def matrix_kernel(c_ref, g_ref, n_ref, m_ref, mat_ref, low_ref, high_ref, last_ref):
    def emit(k, g, n, m):
        g_ref[rows(k), :] = g
        n_ref[rows(k), :] = n
        m_ref[rows(k + 1), :] = m

    cells = [c_ref[turned(k), :] for k in range(N)]
    q, e0, e1 = eliminated(cells, emit)
    for k, part in enumerate((q, e0, e1, cells[0], cells[N - 1])):
        mat_ref[rows(k), :] = part
    size = 64
    lane = lax.broadcasted_iota(jnp.int32, (size, LANES), 1)
    for start in range(0, N * N, size):
        c = c_ref[pl.ds(start, size), :]
        inner = jnp.where(lane < LANES - 1, 0.25 * (c + pltpu.roll(c, LANES - 1, 1)), 0.0)
        lower, upper = pltpu.roll(inner, 1, 1), inner
        excess = jnp.where((lane > 0) & (lane < LANES - 1), 1.0, 1.0 + 0.25 * c)
        for at, s in enumerate(ROUNDS):
            g = 1.0 / (lower + upper + excess)
            lg, ug, eg = lower * g, upper * g, excess * g
            low_ref[pl.ds(at * N * N + start, size), :] = lower * pltpu.roll(g, s, 1)
            high_ref[pl.ds(at * N * N + start, size), :] = upper * pltpu.roll(g, LANES - s, 1)
            excess = excess + lower * pltpu.roll(eg, s, 1) + upper * pltpu.roll(eg, LANES - s, 1)
            lower, upper = lower * pltpu.roll(lg, s, 1), upper * pltpu.roll(ug, LANES - s, 1)
        last_ref[pl.ds(start, size), :] = 1.0 / excess


def x_back_kernel(
    ret_ref, f_ref, gr_ref, n_ref, m_ref, gy_ref, ny_ref, my_ref, mat_ref, gry_ref, pay_ref, u_ref
):
    def emit(k, w):
        u_ref[rows(k), :] = w - 2.0 * f_ref[rows(k), :]

    backward(ret_ref[rows(0), :], ret_ref[rows(1), :], gr_ref, n_ref, m_ref, emit)
    r0, r1 = forward(lambda k: u_ref[turned(k), :], gy_ref, ny_ref, my_ref, gry_ref)
    values = [mat_ref[rows(k), :] for k in range(5)] + [r0, r1, jnp.zeros_like(r0)]
    for k, value in enumerate(values):
        pay_ref[pl.ds(k, N, stride=VALUES), :] = value


def y_back_kernel(
    ret_ref, f_ref, gry_ref, ny_ref, my_ref, low_ref, high_ref, last_ref, out_ref, u_ref
):
    def emit(k, u):
        u_ref[turned(k), :] = u

    backward(
        ret_ref[pl.ds(0, N, stride=2), :], ret_ref[pl.ds(1, N, stride=2), :], gry_ref, ny_ref, my_ref, emit
    )
    right = u_ref[...]
    for at, s in enumerate(ROUNDS):
        part = pl.ds(at * N * N, N * N)
        right = (
            right
            + low_ref[part, :] * pltpu.roll(right, s, 1)
            + high_ref[part, :] * pltpu.roll(right, LANES - s, 1)
        )
    out_ref[...] = f_ref[...] + right * last_ref[...]


def call(kernel, outs, scratch=(), flops=100_000):
    return pl.pallas_call(
        kernel,
        out_shape=outs,
        scratch_shapes=[pltpu.VMEM(dims, jnp.float32) for dims in scratch],
        compiler_params=pltpu.CompilerParams(vmem_limit_bytes=32 * 1024 * 1024),
    )


def body(field, conductance, source):
    size_x, size_y = lax.axis_size("gx"), lax.axis_size("gy")
    cells = N * N
    up = [(i, i + 1) for i in range(size_y - 1)]
    last = jnp.concatenate([field[:, N - 1], conductance[:, N - 1]])
    first = jnp.concatenate([field[:, 0], conductance[:, 0]])
    from_down = lax.ppermute(last, "gy", up)
    from_up = lax.ppermute(first, "gy", [(b, a) for a, b in up])
    f, c, s = (part.reshape(cells, LANES) for part in (field, conductance, source))
    whole = shape(cells, LANES)
    rhs, gx, nx, mx, mat_x = call(
        prepare_kernel, (whole, whole, whole, whole, shape(3 * N, LANES)), [(cells, LANES)]
    )(f, c, s)
    grx, pay = call(x_forward_kernel, (whole, shape(2 * N * VALUES, LANES)), [(cells, LANES)])(
        f, c, rhs, gx, nx, mx, mat_x, from_down, from_up
    )
    got = lax.all_to_all(pay.reshape(size_x, VALUES, LANES), "gx", 0, 0, tiled=True)
    gy, ny, my, mat_y, low, high, final = call(
        matrix_kernel,
        (whole, whole, whole, shape(5 * N, LANES))
        + (shape(len(ROUNDS) * cells, LANES), shape(len(ROUNDS) * cells, LANES), whole),
    )(c)
    solved = call(lambda *refs: x_middle_kernel(size_x, *refs), shape(size_x, LANES))(
        got.reshape(size_x * VALUES, LANES)
    )
    ret = lax.all_to_all(solved.reshape(size_x, 1, LANES), "gx", 0, 0, tiled=True)
    gry, pay = call(x_back_kernel, (whole, shape(N * VALUES, LANES)), [(cells, LANES)])(
        ret.reshape(size_x, LANES), f, grx, nx, mx, gy, ny, my, mat_y
    )
    got = lax.all_to_all(pay.reshape(size_y, VALUES, LANES), "gy", 0, 0, tiled=True)
    solved = call(lambda *refs: y_middle_kernel(size_y, *refs), shape(2 * size_y, LANES))(
        got.reshape(size_y * VALUES, LANES)
    )
    ret = lax.all_to_all(solved.reshape(size_y, 2, LANES), "gy", 0, 0, tiled=True)
    out = call(y_back_kernel, whole, [(cells, LANES)])(
        ret.reshape(2 * size_y, LANES), f, gry, ny, my, low, high, final
    )
    return out.reshape(field.shape)


def solution(mesh):
    spec = P("gx", "gy", None)
    return jax.shard_map(
        body, mesh=mesh, in_specs=(spec, spec, spec), out_specs=spec, check_vma=False
    )
```

time: 148 us -> 76.8 us (0.52); the launches traced: 146 us -> 76.5 us
  waiting for transfers between devices: 55.4 us -> 5.63 us
  blocking collectives: 0 us -> 47.6 us
  other arithmetic: 27.3 us -> 0.01 us
  starting transfers between devices: 35.2 us -> 13.9 us
  local copies, waits for them, and re-layouts: 17.1 us -> 3.62 us
  loops' own time: 9.8 us -> 0 us
  Pallas kernels: 0 us -> 5.53 us
    all_to_all x2 -> x1, waiting for transfers between devices: 54.4 us -> 5.63 us  [body(): lax.all_to_all(solved.reshape(size_x, 1, LANES), 'gx', 0, 0, tiled=True)]
    all_to_all x0 -> x3, blocking collectives: none -> 47.6 us  [the longest x1 19.7 us: body(): lax.all_to_all(pay.reshape(size_x, VALUES, LANES), 'gx', 0, 0, tiled=True)]
    all_to_all x2 -> x1, starting transfers between devices: 22.6 us -> 3.83 us  [body(): lax.all_to_all(solved.reshape(size_x, 1, LANES), 'gx', 0, 0, tiled=True)]
    dynamic_update_slice x340 -> x0, other arithmetic: 16.5 us -> none  [thomas(): lax.scan(forward_step, start, (lower, diag, upper, stacked))]
    another operation x6 -> x0, loops' own time: 9.8 us -> none  [the longest x3 6.46 us: thomas(): lax.scan(forward_step, start, (lower, diag, upper, stacked))]
    pallas_call x0 -> x7, Pallas kernels: none -> 5.53 us  [the longest x1 2.85 us: body(): call(matrix_kernel, (whole, whole, whole, shape(5 * N, LANES)) + (shape(l...]
    dynamic_update_slice x128 -> x0, local copies, waits for them, and re-layouts: 5.52 us -> none  [thomas(): lax.scan(forward_step, start, (lower, diag, upper, stacked))]
    mul x146 -> x0, other arithmetic: 3.69 us -> none  [the longest x128 2.02 us: forward_step(): ratio = upp * inverse]
  transfers between devices with their start and end apart: 6 -> 3, of which waited for: 3 -> 1; matrix products, arithmetic and copies ran while one was open for 5% -> 0% of each run, Pallas kernels for 0% -> 4%
where the time goes in v1:
time: 76.8 us; the launch traced here: 76.5 us
  blocking collectives  47.6 us (62%)
  starting transfers between devices  13.9 us (18%)
  waiting for transfers between devices  5.63 us (7%)
  Pallas kernels  5.53 us (7%)
  local copies, waits for them, and re-layouts  3.62 us (5%)
    all_to_all x1, blocking collectives, body(): lax.all_to_all(pay.reshape(size_x, VALUES, LANES), 'gx', 0, 0, tiled=True)  19.7 us
    all_to_all x1, blocking collectives, body(): lax.all_to_all(pay.reshape(size_y, VALUES, LANES), 'gy', 0, 0, tiled=True)  18 us
    all_to_all x1, blocking collectives, body(): lax.all_to_all(solved.reshape(size_y, 2, LANES), 'gy', 0, 0, tiled=True)  9.96 us
    all_to_all x1, waiting for transfers between devices, body(): lax.all_to_all(solved.reshape(size_x, 1, LANES), 'gx', 0, 0, tiled=True)  5.63 us
    ppermute x1, starting transfers between devices, body(): from_up = lax.ppermute(first, 'gy', [(b, a) for a, b in up])  5.48 us
    ppermute x1, starting transfers between devices, body(): from_down = lax.ppermute(last, 'gy', up)  4.59 us
    all_to_all x1, starting transfers between devices, body(): lax.all_to_all(solved.reshape(size_x, 1, LANES), 'gx', 0, 0, tiled=True)  3.83 us
    pallas_call x1, Pallas kernels, body(): call(matrix_kernel, (whole, whole, whole, shape(5 * N, LANES)) + (shape(l...  2.85 us
  transfers between devices with their start and end apart: 3, of which 1 were waited for; matrix products, arithmetic and copies ran while one was open for 0% of the time, Pallas kernels for 4%

profile of v1, /device:TPU:1, one launch (start us, length us, event | category | flops | bytes accessed | tf_op | source)
XLA Modules:
  0.0 76.5 jit_solution(12079643598521387673)
XLA Ops:
  0.0 0.0 copy-start
  0.0 0.9 %fusion = (f32[16,1,128]{2,1,0:T(1,128)S(1)}, f32[16,1,128]{2,1,0:T(1,128)S(1)}) fusion(f32[16,16,128]{2,1,0:T(8,128)} %param.3), kind=kLoop, calls=%fused_computation.2 | loop fusion | bytes 32768 | tf_op jit(solution)/shard_map/slice | solution.py:232
  0.9 0.9 %fusion.1 = (f32[16,1,128]{2,1,0:T(1,128)S(1)}, f32[16,1,128]{2,1,0:T(1,128)S(1)}) fusion(f32[16,16,128]{2,1,0:T(8,128)} %param.4), kind=kLoop, calls=%fused_computation.3 | loop fusion | bytes 32768 | tf_op jit(solution)/shard_map/slice | solution.py:232
  1.8 4.6 %collective-permute-start = (f32[32,128]{1,0:T(8,128)S(1)}, f32[32,128]{1,0:T(8,128)S(1)}, u32[]{:S(2)}, u32[]{:S(2)}) collective-permute-start(f32[32,128]{1,0:T(8,128)S(1)} %pad_maximum_fusion), channel_id=1, source_target_pairs={{0,1},{1,2},{2,3},{3,4},{4,5},{5,6},{6,7},{7,8},{8,9},{9,10},{10,1... | collective-permute-start | bytes 49160 | tf_op jit(solution)/shard_map/ppermute | solution.py:233
  6.4 5.5 %collective-permute-start.1 = (f32[32,128]{1,0:T(8,128)S(1)}, f32[32,128]{1,0:T(8,128)S(1)}, u32[]{:S(2)}, u32[]{:S(2)}) collective-permute-start(f32[32,128]{1,0:T(8,128)S(1)} %pad_maximum_fusion.1), channel_id=1, source_target_pairs={{1,0},{2,1},{3,2},{4,3},{5,4},{6,5},{7,6},{8,7},{9,8},{10,9},{11,1... | collective-permute-start | bytes 49160 | tf_op jit(solution)/shard_map/ppermute | solution.py:234
  11.9 0.0 copy-done
  11.9 0.0 copy-start.1
  12.0 0.9 %copy-done.1 = f32[16,16,128]{2,1,0:T(8,128)S(1)} copy-done((f32[16,16,128]{2,1,0:T(8,128)S(1)}, f32[16,16,128]{2,1,0:T(8,128)}, u32[]{:S(2)}) %copy-start.1) | copy-done | bytes 131096
  12.9 0.0 copy-start.3
  12.9 0.9 %copy-done.3 = f32[16,16,128]{2,1,0:T(8,128)S(1)} copy-done((f32[16,16,128]{2,1,0:T(8,128)S(1)}, f32[16,16,128]{2,1,0:T(8,128)}, u32[]{:S(2)}) %copy-start.3) | copy-done | bytes 131096
  13.8 0.3 shard_map.37
  14.0 0.0 collective-permute-done.down_ref
  14.0 0.0 collective-permute-done.1.up_ref
  14.0 0.1 shard_map.38
  14.1 19.7 %all_to_all.20 = f32[32,8,128]{2,1,0:T(8,128)S(1)} all-to-all(f32[32,8,128]{2,1,0:T(8,128)S(1)} %bitcast.36), channel_id=1, replica_groups=mesh['gx'=32,'gy'=16] {'gx'}, dimensions={0} | all-to-all | bytes 262144 | tf_op jit(solution)/shard_map/all_to_all | solution.py:243
  33.8 0.0 copy-start.2
  33.8 0.7 shard_map.39
  34.5 3.8 %all-to-all-start.1 = ((f32[32,1,128]{2,1,0:T(1,128)}), f32[32,1,128]{2,1,0:T(1,128)S(1)}, u32[]{:S(2)}, u32[]{:S(2)}) async-start(f32[32,1,128]{2,1,0:T(1,128)} %bitcast.10), calls=%async_computation.1 | async-start | bytes 32768 | tf_op jit(solution)/shard_map/all_to_all | solution.py:252
  38.4 0.0 copy-done.2
  38.4 2.9 %shard_map.40 = (f32[256,128]{1,0:T(8,128)S(1)}, f32[256,128]{1,0:T(8,128)S(1)}, f32[256,128]{1,0:T(8,128)S(1)}, f32[80,128]{1,0:T(8,128)S(1)}, f32[1792,128]{1,...) custom-call(f32[256,128]{1,0:T(8,128)S(1)} %bitcast.32), custom_call_target="tpu_custom_call" | custom-call | tf_op jit(solution)/shard_map/pallas_call | solution.py:244
  41.2 5.6 %all-to-all-done.1 = f32[32,1,128]{2,1,0:T(1,128)S(1)} async-done(((f32[32,1,128]{2,1,0:T(1,128)}), f32[32,1,128]{2,1,0:T(1,128)S(1)}, u32[]{:S(2)}, u32[]{:S(2)}) %all-to-all-start.1) | async-done | bytes 16416 | tf_op jit(solution)/shard_map/all_to_all | solution.py:252
  46.9 0.1 shard_map.41
  47.0 18.0 %all_to_all.21 = f32[16,8,128]{2,1,0:T(8,128)S(1)} all-to-all(f32[16,8,128]{2,1,0:T(8,128)S(1)} %bitcast.40), channel_id=1, replica_groups=mesh['gx'=32,'gy'=16] {'gy'}, dimensions={0} | all-to-all | bytes 131072 | tf_op jit(solution)/shard_map/all_to_all | solution.py:256
  65.0 0.1 shard_map.42
  65.1 10.0 %all_to_all.22 = f32[16,2,128]{2,1,0:T(2,128)S(1)} all-to-all(f32[16,2,128]{2,1,0:T(2,128)S(1)} %bitcast.39), channel_id=1, replica_groups=mesh['gx'=32,'gy'=16] {'gy'}, dimensions={0} | all-to-all | bytes 32768 | tf_op jit(solution)/shard_map/all_to_all | solution.py:260
  75.0 1.4 %shard_map.43 = f32[256,128]{1,0:T(8,128)} custom-call(f32[32,128]{1,0:T(8,128)S(1)} %bitcast.38, f32[256,128]{1,0:T(8,128)S(1)} %bitcast.29, f32[256,128]{1,0:T(8,128)S(1)} %get-tuple-element.33.gry_ref, f32[256,128]{1,0:T(8,128)S(1)} %get-tuple-element.29.ny_ref, f32[256,128]{1,0:T(8,128)S(1)} %get-tuple-element.30.my_ref, ...), custom_call_target="tpu_custom_call" | custom-call | tf_op jit(solution)/shard_map/pallas_call | solution.py:261
  (2 shorter events, 0.0 us)
Async XLA Ops:
  0.0 11.9 %copy-start = (f32[16,16,128]{2,1,0:T(8,128)S(1)}, f32[16,16,128]{2,1,0:T(8,128)}, u32[]{:S(2)}) copy-start(f32[16,16,128]{2,1,0:T(8,128)} %param.3) | copy-start | bytes 393220
  1.8 12.2 %collective-permute-start = (f32[32,128]{1,0:T(8,128)S(1)}, f32[32,128]{1,0:T(8,128)S(1)}, u32[]{:S(2)}, u32[]{:S(2)}) collective-permute-start(f32[32,128]{1,0:T(8,128)S(1)} %pad_maximum_fusion), channel_id=1, source_target_pairs={{0,1},{1,2},{2,3},{3,4},{4,5},{5,6},{6,7},{7,8},{8,9},{9,10},{10,1... | collective-permute-start | bytes 49160 | tf_op jit(solution)/shard_map/ppermute | solution.py:233
  6.4 7.6 %collective-permute-start.1 = (f32[32,128]{1,0:T(8,128)S(1)}, f32[32,128]{1,0:T(8,128)S(1)}, u32[]{:S(2)}, u32[]{:S(2)}) collective-permute-start(f32[32,128]{1,0:T(8,128)S(1)} %pad_maximum_fusion.1), channel_id=1, source_target_pairs={{1,0},{2,1},{3,2},{4,3},{5,4},{6,5},{7,6},{8,7},{9,8},{10,9},{11,1... | collective-permute-start | bytes 49160 | tf_op jit(solution)/shard_map/ppermute | solution.py:234
  11.9 0.9 %copy-start.1 = (f32[16,16,128]{2,1,0:T(8,128)S(1)}, f32[16,16,128]{2,1,0:T(8,128)}, u32[]{:S(2)}) copy-start(f32[16,16,128]{2,1,0:T(8,128)} %param.4) | copy-start | bytes 393220
  12.9 0.9 %copy-start.3 = (f32[16,16,128]{2,1,0:T(8,128)S(1)}, f32[16,16,128]{2,1,0:T(8,128)}, u32[]{:S(2)}) copy-start(f32[16,16,128]{2,1,0:T(8,128)} %param.5) | copy-start | bytes 393220
  33.8 4.6 %copy-start.2 = (f32[16,16,128]{2,1,0:T(8,128)S(1)}, f32[16,16,128]{2,1,0:T(8,128)}, u32[]{:S(2)}) copy-start(f32[16,16,128]{2,1,0:T(8,128)} %param.4) | copy-start | bytes 393220
  34.5 12.3 %all-to-all-start.1 = ((f32[32,1,128]{2,1,0:T(1,128)}), f32[32,1,128]{2,1,0:T(1,128)S(1)}, u32[]{:S(2)}, u32[]{:S(2)}) async-start(f32[32,1,128]{2,1,0:T(1,128)} %bitcast.10), calls=%async_computation.1 | async-start | bytes 32768 | tf_op jit(solution)/shard_map/all_to_all | solution.py:252

commit v2 on v1

v2 whole, which is shorter than its diff:
```python
import jax
import jax.numpy as jnp
from jax import lax
from jax.experimental import pallas as pl
from jax.experimental.pallas import tpu as pltpu
from jax.sharding import PartitionSpec as P

N = 16
CELLS = N * N
LANES = 128
ROUNDS = (1, 2, 4, 8, 16, 32, 64)
RING_X = 4
CORES = 2


def rows(k):
    return pl.ds(N * k, N)


def turned(k):
    return pl.ds(k, N, stride=N)


def shape(*dims):
    return jax.ShapeDtypeStruct(dims, jnp.float32)


def eliminated(cells, g_ref, n_ref, m_ref):
    one = jnp.ones_like(cells[0])
    half = [None] + [0.25 * (cells[k - 1] + cells[k]) for k in range(1, N)]
    first, excess, excess_first = half[1], one, one
    for k in range(1, N - 1):
        g = 1.0 / (first + half[k + 1] + excess)
        n = first * g
        m = half[k + 1] * g
        g_ref[rows(k), :] = g
        n_ref[rows(k), :] = n
        m_ref[rows(k + 1), :] = m
        excess_first = excess_first + n * excess
        first = m * first
        excess = one + m * excess
    return first, excess_first, excess


def forward(right, g_ref, n_ref, m_ref, gr_ref):
    r0, carried = right(0), None
    for k in range(1, N):
        carried = right(k) if carried is None else right(k) + m_ref[rows(k), :] * carried
        if k < N - 1:
            r0 = r0 + n_ref[rows(k), :] * carried
            gr_ref[rows(k), :] = g_ref[rows(k), :] * carried
    return r0, carried


def backward(u0, u1, gr_ref, n_ref, m_ref, emit):
    emit(0, u0)
    emit(N - 1, u1)
    later = u1
    for k in range(N - 2, 0, -1):
        later = gr_ref[rows(k), :] + n_ref[rows(k), :] * u0 + m_ref[rows(k + 1), :] * later
        emit(k, later)


def join_blocks(left, right):
    ql, e0l, e1l, c0l, c1l, r0l, r1l = left
    qr, e0r, e1r, c0r, c1r, r0r, r1r = right
    face = 0.25 * (c1l + c0r)
    h = 1.0 / (ql + face + e1l)
    s, t = face * h, ql * h
    p = s * ql
    ew = e0r + s * e1l
    rw = r0r + s * r1l
    k = 1.0 / (qr + p + ew)
    qk, pk = qr * k, p * k
    joined = (
        qk * p, e0l + t * e1l + pk * ew, e1r + qk * ew, c0l, c1r, r0l + t * r1l + pk * rw, r1r + qk * rw
    )

    def expand(u0, u1):
        w = k * rw + qk * u1 + pk * u0
        return (u0, h * r1l + t * u0 + s * w), (w, u1)

    return joined, expand


def join_elements(left, right):
    kl, eal, ebl, ral, rbl = left
    kr, ear, ebr, rar, rbr = right
    em, rm = ebl + ear, rbl + rar
    k = 1.0 / (kl + kr + em)
    lk, rk = kl * k, kr * k
    joined = (lk * kr, eal + lk * em, ebr + rk * em, ral + lk * rm, rbr + rk * rm)

    def expand(u0, u1):
        middle = k * rm + lk * u0 + rk * u1
        return (u0, middle), (middle, u1)

    return joined, expand


def tree(parts, join):
    levels = []
    while len(parts) > 1:
        pairs = [join(parts[i], parts[i + 1]) for i in range(0, len(parts), 2)]
        levels.append([expand for _, expand in pairs])
        parts = [joined for joined, _ in pairs]

    def ends(u0, u1):
        found = [(u0, u1)]
        for expands in reversed(levels):
            found = [end for expand, both in zip(expands, found) for end in expand(*both)]
        return found

    return parts[0], ends


def chosen(found, scratch_ref, index):
    for i, (u0, u1) in enumerate(found):
        scratch_ref[rows(2 * i), :] = u0
        scratch_ref[rows(2 * i + 1), :] = u1
    return (
        scratch_ref[pl.ds(pl.multiple_of(index * 2 * N, 2 * N), N), :],
        scratch_ref[pl.ds(pl.multiple_of(index * 2 * N, 2 * N) + N, N), :],
    )


def parts_of(ref, i, count):
    return tuple(ref[rows(count * i + k), :] for k in range(count))


def replicate(pay_ref, values, copies):
    for i in range(copies):
        for k, value in enumerate(values):
            pay_ref[rows(len(values) * i + k), :] = value


def prepare_kernel(
    all_ref, f_ref, c_ref, last_ref, first_ref, rhs_ref, g_ref, n_ref, m_ref, mat_ref, ay_ref
):
    f_ref[...] = all_ref[pl.ds(0, CELLS), :]
    c_ref[...] = all_ref[pl.ds(CELLS, CELLS), :]
    for edge_ref, y in ((first_ref, 0), (last_ref, N - 1)):
        edge_ref[rows(0), :] = all_ref[turned(y), :]
        edge_ref[rows(1), :] = all_ref[pl.ds(CELLS + y, N, stride=N), :]
    cells = [all_ref[rows(N + k), :] for k in range(N)]
    for k, part in enumerate(eliminated(cells, g_ref, n_ref, m_ref)):
        mat_ref[rows(k), :] = part
    flux = None
    for y in range(N - 1):
        c0, c1 = c_ref[turned(y), :], c_ref[turned(y + 1), :]
        f0, f1 = f_ref[turned(y), :], f_ref[turned(y + 1), :]
        after = 0.5 * (c0 + c1) * (f1 - f0)
        ay_ref[turned(y), :] = after if flux is None else after - flux
        flux = after
    ay_ref[turned(N - 1), :] = -flux
    lane = lax.broadcasted_iota(jnp.int32, (N, LANES), 1)
    for k in range(N):
        c, f = cells[k], f_ref[rows(k), :]
        c_next = jnp.where(lane < LANES - 1, pltpu.roll(c, LANES - 1, 1), 0.0)
        f_next = jnp.where(lane < LANES - 1, pltpu.roll(f, LANES - 1, 1), 0.0)
        upper = 0.5 * (c + c_next) * (f_next - f)
        lower = jnp.where(lane > 0, pltpu.roll(upper, 1, 1), 0.5 * c * f)
        rhs_ref[rows(k), :] = 2.0 * f + all_ref[rows(2 * N + k), :] + ay_ref[rows(k), :] + (upper - lower)


def x_forward_kernel(
    f_ref, c_ref, rhs_ref, g_ref, n_ref, m_ref, mat_ref, maty_ref, down_ref, up_ref, gr_ref, pay_ref, elem_ref, r_ref
):
    r_ref[...] = rhs_ref[...]
    flux_down = 0.5 * (down_ref[rows(1), :] + c_ref[turned(0), :]) * (
        f_ref[turned(0), :] - down_ref[rows(0), :]
    )
    flux_up = 0.5 * (up_ref[rows(1), :] + c_ref[turned(N - 1), :]) * (
        up_ref[rows(0), :] - f_ref[turned(N - 1), :]
    )
    r_ref[turned(0), :] = r_ref[turned(0), :] - flux_down
    r_ref[turned(N - 1), :] = r_ref[turned(N - 1), :] + flux_up
    r0, r1 = forward(lambda k: r_ref[rows(k), :], g_ref, n_ref, m_ref, gr_ref)
    values = [mat_ref[rows(k), :] for k in range(3)]
    replicate(pay_ref, values + [c_ref[rows(0), :], c_ref[rows(N - 1), :], r0, r1], RING_X)
    q, e0, e1 = parts_of(maty_ref, 0, 3)
    face = 0.25 * (c_ref[turned(N - 1), :] + up_ref[rows(1), :])
    e0 = e0 + jnp.where(lax.axis_index("gy") == 0, 0.25 * c_ref[turned(0), :], 0.0)
    h = 1.0 / (q + face + e1)
    qh, fh = q * h, face * h
    replicate(elem_ref, (qh * face, e0 + qh * e1, fh * e1, qh, fh, h), 1)


def x_merge_kernel(rings, got_ref, pay_ref):
    whole, _ = tree([parts_of(got_ref, i, 7) for i in range(RING_X)], join_blocks)
    replicate(pay_ref, whole, rings)


def matrix_kernel(c_ref, g_ref, n_ref, m_ref, mat_ref, low_ref, high_ref, last_ref):
    cells = [c_ref[turned(k), :] for k in range(N)]
    for k, part in enumerate(eliminated(cells, g_ref, n_ref, m_ref)):
        mat_ref[rows(k), :] = part
    size = 64
    lane = lax.broadcasted_iota(jnp.int32, (size, LANES), 1)
    for start in range(0, CELLS, size):
        c = c_ref[pl.ds(start, size), :]
        inner = jnp.where(lane < LANES - 1, 0.25 * (c + pltpu.roll(c, LANES - 1, 1)), 0.0)
        lower, upper = pltpu.roll(inner, 1, 1), inner
        excess = jnp.where((lane > 0) & (lane < LANES - 1), 1.0, 1.0 + 0.25 * c)
        for at, s in enumerate(ROUNDS):
            g = 1.0 / (lower + upper + excess)
            lg, ug, eg = lower * g, upper * g, excess * g
            low_ref[pl.ds(at * CELLS + start, size), :] = lower * pltpu.roll(g, s, 1)
            high_ref[pl.ds(at * CELLS + start, size), :] = upper * pltpu.roll(g, LANES - s, 1)
            excess = excess + lower * pltpu.roll(eg, s, 1) + upper * pltpu.roll(eg, LANES - s, 1)
            lower, upper = lower * pltpu.roll(lg, s, 1), upper * pltpu.roll(ug, LANES - s, 1)
        last_ref[pl.ds(start, size), :] = 1.0 / excess


def x_back_kernel(
    rings, ring_ref, all_ref, f_ref, gr_ref, n_ref, m_ref, gy_ref, ny_ref, my_ref, mat_ref, gry_ref, pay_ref, hr_ref, u_ref, ends_ref
):
    me = lax.axis_index("gx")
    whole, ends = tree([parts_of(all_ref, i, 7) for i in range(rings)], join_blocks)
    q, e0, e1, c0, c1, r0, r1 = whole
    e0, e1 = e0 + 0.25 * c0, e1 + 0.25 * c1
    h = 1.0 / (q + e1)
    qh = q * h
    u0 = (r0 + qh * r1) / (e0 + qh * e1)
    u0, u1 = chosen(ends(u0, h * r1 + qh * u0), ends_ref, me // RING_X)
    _, ends = tree([parts_of(ring_ref, i, 7) for i in range(RING_X)], join_blocks)
    u0, u1 = chosen(ends(u0, u1), ends_ref, me % RING_X)

    def emit(k, w):
        u_ref[rows(k), :] = w - 2.0 * f_ref[rows(k), :]

    backward(u0, u1, gr_ref, n_ref, m_ref, emit)
    r0, r1 = forward(lambda k: u_ref[turned(k), :], gy_ref, ny_ref, my_ref, gry_ref)
    kappa, ea, eb, qh, fh, h = parts_of(mat_ref, 0, 6)
    replicate(pay_ref, (kappa, ea, eb, r0 + qh * r1, fh * r1), 1)
    hr_ref[...] = h * r1


def core_pair(own_ref, other_ref):
    odd = lax.axis_index("gy") % CORES == 1
    own, other = parts_of(own_ref, 0, 5), parts_of(other_ref, 0, 5)
    low = tuple(jnp.where(odd, b, a) for a, b in zip(own, other))
    high = tuple(jnp.where(odd, a, b) for a, b in zip(own, other))
    return join_elements(low, high)


def y_merge_kernel(rings, own_ref, other_ref, pay_ref):
    whole, _ = core_pair(own_ref, other_ref)
    replicate(pay_ref, whole, rings)


def y_back_kernel(
    rings, all_ref, own_ref, other_ref, mat_ref, hr_ref, f_ref, gry_ref, ny_ref, my_ref, low_ref, high_ref, last_ref, out_ref, u_ref, ends_ref
):
    me = lax.axis_index("gy")
    (kappa, ea, _, ra, _), ends = tree([parts_of(all_ref, i, 5) for i in range(rings)], join_elements)
    u0 = ra / (kappa + ea)
    u0, u1 = chosen(ends(u0, jnp.zeros_like(u0)), ends_ref, me // CORES)
    _, expand = core_pair(own_ref, other_ref)
    u0, u_next = chosen(expand(u0, u1), ends_ref, me % CORES)
    u1 = hr_ref[...] + mat_ref[rows(3), :] * u0 + mat_ref[rows(4), :] * u_next

    def emit(k, u):
        u_ref[turned(k), :] = u

    backward(u0, u1, gry_ref, ny_ref, my_ref, emit)
    right = u_ref[...]
    for at, s in enumerate(ROUNDS):
        part = pl.ds(at * CELLS, CELLS)
        right = (
            right
            + low_ref[part, :] * pltpu.roll(right, s, 1)
            + high_ref[part, :] * pltpu.roll(right, LANES - s, 1)
        )
    out_ref[...] = f_ref[...] + right * last_ref[...]


def call(kernel, outs, scratch=()):
    return pl.pallas_call(
        kernel,
        out_shape=outs,
        scratch_shapes=[pltpu.VMEM(part, jnp.float32) for part in scratch],
        compiler_params=pltpu.CompilerParams(vmem_limit_bytes=16 * 1024 * 1024),
    )


def gathered(pay, axis, groups):
    count = len(groups[0])
    got = lax.all_to_all(
        pay.reshape(count, -1, LANES), axis, 0, 0, tiled=True, axis_index_groups=groups
    )
    return got.reshape(-1, LANES)


def body(field, conductance, source):
    size_x, size_y = lax.axis_size("gx"), lax.axis_size("gy")
    rings_x, rings_y = size_x // RING_X, size_y // CORES
    f, c, s = (part.reshape(CELLS, LANES) for part in (field, conductance, source))
    whole, block = shape(CELLS, LANES), (CELLS, LANES)
    f, c, last, first, rhs, gx, nx, mx, mat_x = call(
        prepare_kernel,
        (whole, whole, shape(2 * N, LANES), shape(2 * N, LANES), whole, whole, whole, whole, shape(3 * N, LANES)),
        [block],
    )(jnp.concatenate([f, c, s]))
    up = [(i, i + 1) for i in range(size_y - 1)]
    from_down = lax.ppermute(last, "gy", up)
    from_up = lax.ppermute(first, "gy", [(b, a) for a, b in up])
    coefficients = shape(len(ROUNDS) * CELLS, LANES)
    gy, ny, my, mat_y, low, high, final = call(
        matrix_kernel, (whole, whole, whole, shape(3 * N, LANES), coefficients, coefficients, whole)
    )(c)
    grx, pay, mat_y = call(
        x_forward_kernel, (whole, shape(RING_X * 7 * N, LANES), shape(6 * N, LANES)), [block]
    )(f, c, rhs, gx, nx, mx, mat_x, mat_y, from_down, from_up)
    ring = gathered(pay, "gx", [[RING_X * i + j for j in range(RING_X)] for i in range(rings_x)])
    pay = call(lambda *refs: x_merge_kernel(rings_x, *refs), shape(rings_x * 7 * N, LANES))(ring)
    every = gathered(pay, "gx", [[RING_X * i + j for i in range(rings_x)] for j in range(RING_X)])
    gry, own, hr = call(
        lambda *refs: x_back_kernel(rings_x, *refs),
        (whole, shape(5 * N, LANES), shape(N, LANES)),
        [block, (2 * max(rings_x, RING_X) * N, LANES)],
    )(ring, every, f, grx, nx, mx, gy, ny, my, mat_y)
    other = lax.ppermute(own, "gy", [(i, i ^ 1) for i in range(size_y)])
    pay = call(lambda *refs: y_merge_kernel(rings_y, *refs), shape(rings_y * 5 * N, LANES))(own, other)
    every = gathered(pay, "gy", [[CORES * i + j for i in range(rings_y)] for j in range(CORES)])
    out = call(
        lambda *refs: y_back_kernel(rings_y, *refs), whole, [block, (2 * rings_y * N, LANES)]
    )(every, own, other, mat_y, hr, f, gry, ny, my, low, high, final)
    return out.reshape(field.shape)


def solution(mesh):
    spec = P("gx", "gy", None)
    return jax.shard_map(
        body, mesh=mesh, in_specs=(spec, spec, spec), out_specs=spec, check_vma=False
    )
```

time: 76.8 us -> 71.7 us (0.934)
  waiting for transfers between devices: 5.63 us -> 0.85 us
  blocking collectives: 47.6 us -> 51.9 us
  local copies, waits for them, and re-layouts: 3.62 us -> 0 us
  starting transfers between devices: 13.9 us -> 12.4 us
  other arithmetic: 0.01 us -> 1.06 us
    all_to_all x1 -> x0, waiting for transfers between devices: 5.63 us -> none  [body(): lax.all_to_all(solved.reshape(size_x, 1, LANES), 'gx', 0, 0, tiled=True)]
    all_to_all x3, blocking collectives: 47.6 us -> 51.9 us  [gathered(): lax.all_to_all(pay.reshape(count, -1, LANES), axis, 0, 0, tiled=True, axi...]
    all_to_all x1 -> x0, starting transfers between devices: 3.83 us -> none  [body(): lax.all_to_all(solved.reshape(size_x, 1, LANES), 'gx', 0, 0, tiled=True)]
    ppermute x0 -> x1, starting transfers between devices: none -> 2.33 us  [body(): other = lax.ppermute(own, 'gy', [(i, i ^ 1) for i in range(size_y)])]
    slice x2 -> x0, local copies, waits for them, and re-layouts: 1.81 us -> none  [body(): first = jnp.concatenate([field[:, 0], conductance[:, 0]])]
    unnamed x8 -> x0, local copies, waits for them, and re-layouts: 1.81 us -> none
    concatenate x2 -> x1, other arithmetic: 0.01 us -> 1.06 us  [body(): jnp.concatenate([f, c, s])]
    ppermute x0 -> x1, waiting for transfers between devices: none -> 0.85 us  [body(): other = lax.ppermute(own, 'gy', [(i, i ^ 1) for i in range(size_y)])]
where the time goes in v2:
time: 71.7 us; the launch traced here: 71.4 us
  blocking collectives  51.9 us (72%)
  starting transfers between devices  12.4 us (17%)
  Pallas kernels  5.05 us (7%)
  other arithmetic  1.06 us (1%)
  waiting for transfers between devices  0.85 us (1%)
    all_to_all x3, blocking collectives, gathered(): lax.all_to_all(pay.reshape(count, -1, LANES), axis, 0, 0, tiled=True, axi...  51.9 us
    ppermute x1, starting transfers between devices, body(): from_up = lax.ppermute(first, 'gy', [(b, a) for a, b in up])  5.48 us
    ppermute x1, starting transfers between devices, body(): from_down = lax.ppermute(last, 'gy', up)  4.59 us
    pallas_call x1, Pallas kernels, body(): call(matrix_kernel, (whole, whole, whole, shape(3 * N, LANES), coefficien...  2.85 us
    ppermute x1, starting transfers between devices, body(): other = lax.ppermute(own, 'gy', [(i, i ^ 1) for i in range(size_y)])  2.33 us
    pallas_call x1, Pallas kernels, body(): call(lambda *refs: y_back_kernel(rings_y, *refs), whole, [block, (2 * rin...  1.52 us
  transfers between devices with their start and end apart: 3, of which 1 were waited for; matrix products, arithmetic and copies ran while one was open for 0% of the time, Pallas kernels for 4%

profile of v2, /device:TPU:1, one launch (start us, length us, event | category | flops | bytes accessed | tf_op | source)
XLA Modules:
  0.0 71.4 jit_solution(4389025085737684384)
XLA Ops:
  0.0 1.1 %pad_maximum_fusion.all_ref = f32[768,128]{1,0:T(8,128)S(1)} fusion(f32[256,128]{1,0:T(8,128)} %bitcast.17, f32[256,128]{1,0:T(8,128)} %bitcast.18, f32[256,128]{1,0:T(8,128)} %bitcast.19), kind=kLoop, calls=%fused_computation | loop fusion | flops 196608 | bytes 786432 | tf_op jit(solution)/shard_map/concatenate | solution.py:304
  1.1 0.3 shard_map.37
  1.3 4.6 %collective-permute-start = (f32[32,128]{1,0:T(8,128)S(1)}, f32[32,128]{1,0:T(8,128)S(1)}, u32[]{:S(2)}, u32[]{:S(2)}) collective-permute-start(f32[32,128]{1,0:T(8,128)S(1)} %get-tuple-element.35), channel_id=1, source_target_pairs={{0,1},{1,2},{2,3},{3,4},{4,5},{5,6},{6,7},{7,8},{8,9},{9,10},{10,1... | collective-permute-start | bytes 49160 | tf_op jit(solution)/shard_map/ppermute | solution.py:306
  5.9 5.5 %collective-permute-start.1 = (f32[32,128]{1,0:T(8,128)S(1)}, f32[32,128]{1,0:T(8,128)S(1)}, u32[]{:S(2)}, u32[]{:S(2)}) collective-permute-start(f32[32,128]{1,0:T(8,128)S(1)} %get-tuple-element.36), channel_id=1, source_target_pairs={{1,0},{2,1},{3,2},{4,3},{5,4},{6,5},{7,6},{8,7},{9,8},{10,9},{11,1... | collective-permute-start | bytes 49160 | tf_op jit(solution)/shard_map/ppermute | solution.py:307
  11.4 2.9 %shard_map.38 = (f32[256,128]{1,0:T(8,128)S(1)}, f32[256,128]{1,0:T(8,128)S(1)}, f32[256,128]{1,0:T(8,128)S(1)}, f32[48,128]{1,0:T(8,128)S(1)}, f32[1792,128]{1,...) custom-call(f32[256,128]{1,0:T(8,128)S(1)} %get-tuple-element.28.c_ref), custom_call_target="tpu_custom_call" | custom-call | tf_op jit(solution)/shard_map/pallas_call | solution.py:309
  14.3 0.0 collective-permute-done.down_ref
  14.3 0.0 collective-permute-done.1.up_ref
  14.3 0.1 shard_map.39
  14.4 8.9 %all_to_all.15 = f32[4,112,128]{2,1,0:T(8,128)S(1)} all-to-all(f32[4,112,128]{2,1,0:T(8,128)S(1)} %bitcast.16), channel_id=1, replica_groups={{0,16,32,48},{64,80,96,112},{128,144,160,176},{192,208,224,240},{256,27..., dimensions={0} | all-to-all | bytes 458752 | tf_op jit(solution)/shard_map/all_to_all | solution.py:289
  23.3 0.1 shard_map.40
  23.4 23.4 %all_to_all.16 = f32[8,112,128]{2,1,0:T(8,128)S(1)} all-to-all(f32[8,112,128]{2,1,0:T(8,128)S(1)} %bitcast.13), channel_id=1, replica_groups={{0,64,128,192,256,320,384,448},{16,80,144,208,272,336,400,464},{32,96,1..., dimensions={0} | all-to-all | bytes 917504 | tf_op jit(solution)/shard_map/all_to_all | solution.py:289
  46.8 0.2 shard_map.41
  47.0 2.3 %collective-permute-start.2 = (f32[80,128]{1,0:T(8,128)S(1)}, f32[80,128]{1,0:T(8,128)S(1)}, u32[]{:S(2)}, u32[]{:S(2)}) collective-permute-start(f32[80,128]{1,0:T(8,128)S(1)} %get-tuple-element.43.refs_0_.refs_1_), channel_id=1, source_target_pairs={{0,1},{1,0},{2,3},{3,2},{4,5},{5,4},{6,7},{7,6},{8,9},{9,8},{10,11... | collective-permute-start | bytes 122888 | tf_op jit(solution)/shard_map/ppermute | solution.py:323
  49.3 0.8 %collective-permute-done.2.refs_1_.refs_2_ = f32[80,128]{1,0:T(8,128)S(1)} collective-permute-done((f32[80,128]{1,0:T(8,128)S(1)}, f32[80,128]{1,0:T(8,128)S(1)}, u32[]{:S(2)}, u32[]{:S(2)}) %collective-permute-start.2) | collective-permute-done | bytes 40992 | tf_op jit(solution)/shard_map/ppermute | solution.py:323
  50.2 19.6 %all_to_all.17 = f32[8,80,128]{2,1,0:T(8,128)S(1)} all-to-all(f32[8,80,128]{2,1,0:T(8,128)S(1)} %bitcast.15), channel_id=1, replica_groups={{0,2,4,6,8,10,12,14},{1,3,5,7,9,11,13,15},{16,18,20,22,24,26,28,30},{17..., dimensions={0} | all-to-all | bytes 655360 | tf_op jit(solution)/shard_map/all_to_all | solution.py:289
  69.9 1.5 %shard_map.43 = f32[256,128]{1,0:T(8,128)} custom-call(f32[640,128]{1,0:T(8,128)S(1)} %bitcast.14, f32[80,128]{1,0:T(8,128)S(1)} %get-tuple-element.43.refs_0_.refs_1_, f32[80,128]{1,0:T(8,128)S(1)} %collective-permute-done.2.refs_1_.refs_2_, f32[96,128]{1,0:T(8,128)S(1)} %get-tuple-element.42.refs_9_.refs_3_, f32[16,128]{1,0:T(8,128)S(1)} %get-tuple-element.44.refs_4_, ...), custom_call_target="tpu_custom_call" | custom-call | tf_op jit(solution)/shard_map/pallas_call | solution.py:326
  (1 shorter events, 0.0 us)
Async XLA Ops:
  1.3 13.0 %collective-permute-start = (f32[32,128]{1,0:T(8,128)S(1)}, f32[32,128]{1,0:T(8,128)S(1)}, u32[]{:S(2)}, u32[]{:S(2)}) collective-permute-start(f32[32,128]{1,0:T(8,128)S(1)} %get-tuple-element.35), channel_id=1, source_target_pairs={{0,1},{1,2},{2,3},{3,4},{4,5},{5,6},{6,7},{7,8},{8,9},{9,10},{10,1... | collective-permute-start | bytes 49160 | tf_op jit(solution)/shard_map/ppermute | solution.py:306
  5.9 8.4 %collective-permute-start.1 = (f32[32,128]{1,0:T(8,128)S(1)}, f32[32,128]{1,0:T(8,128)S(1)}, u32[]{:S(2)}, u32[]{:S(2)}) collective-permute-start(f32[32,128]{1,0:T(8,128)S(1)} %get-tuple-element.36), channel_id=1, source_target_pairs={{1,0},{2,1},{3,2},{4,3},{5,4},{6,5},{7,6},{8,7},{9,8},{10,9},{11,1... | collective-permute-start | bytes 49160 | tf_op jit(solution)/shard_map/ppermute | solution.py:307
  47.0 3.2 %collective-permute-start.2 = (f32[80,128]{1,0:T(8,128)S(1)}, f32[80,128]{1,0:T(8,128)S(1)}, u32[]{:S(2)}, u32[]{:S(2)}) collective-permute-start(f32[80,128]{1,0:T(8,128)S(1)} %get-tuple-element.43.refs_0_.refs_1_), channel_id=1, source_target_pairs={{0,1},{1,0},{2,3},{3,2},{4,5},{5,4},{6,7},{7,6},{8,9},{9,8},{10,11... | collective-permute-start | bytes 122888 | tf_op jit(solution)/shard_map/ppermute | solution.py:323

commit v3 on v2

--- a/solution.py
+++ b/solution.py
@@ -9,8 +9,8 @@
 CELLS = N * N
 LANES = 128
 ROUNDS = (1, 2, 4, 8, 16, 32, 64)
-RING_X = 4
-CORES = 2
+NEAR_X = 8
+NEAR_Y = 4
 
 
 def rows(k):
@@ -177,7 +177,7 @@
     r_ref[turned(N - 1), :] = r_ref[turned(N - 1), :] + flux_up
     r0, r1 = forward(lambda k: r_ref[rows(k), :], g_ref, n_ref, m_ref, gr_ref)
     values = [mat_ref[rows(k), :] for k in range(3)]
-    replicate(pay_ref, values + [c_ref[rows(0), :], c_ref[rows(N - 1), :], r0, r1], RING_X)
+    replicate(pay_ref, values + [c_ref[rows(0), :], c_ref[rows(N - 1), :], r0, r1], NEAR_X)
     q, e0, e1 = parts_of(maty_ref, 0, 3)
     face = 0.25 * (c_ref[turned(N - 1), :] + up_ref[rows(1), :])
     e0 = e0 + jnp.where(lax.axis_index("gy") == 0, 0.25 * c_ref[turned(0), :], 0.0)
@@ -186,9 +186,9 @@
     replicate(elem_ref, (qh * face, e0 + qh * e1, fh * e1, qh, fh, h), 1)
 
 
-def x_merge_kernel(rings, got_ref, pay_ref):
-    whole, _ = tree([parts_of(got_ref, i, 7) for i in range(RING_X)], join_blocks)
-    replicate(pay_ref, whole, rings)
+def x_merge_kernel(far, got_ref, pay_ref):
+    whole, _ = tree([parts_of(got_ref, i, 7) for i in range(NEAR_X)], join_blocks)
+    replicate(pay_ref, whole, far)
 
 
 def matrix_kernel(c_ref, g_ref, n_ref, m_ref, mat_ref, low_ref, high_ref, last_ref):
@@ -213,18 +213,18 @@
 
 
 def x_back_kernel(
-    rings, ring_ref, all_ref, f_ref, gr_ref, n_ref, m_ref, gy_ref, ny_ref, my_ref, mat_ref, gry_ref, pay_ref, hr_ref, u_ref, ends_ref
+    far, near_ref, all_ref, f_ref, gr_ref, n_ref, m_ref, gy_ref, ny_ref, my_ref, mat_ref, gry_ref, pay_ref, hr_ref, u_ref, ends_ref
 ):
     me = lax.axis_index("gx")
-    whole, ends = tree([parts_of(all_ref, i, 7) for i in range(rings)], join_blocks)
+    whole, ends = tree([parts_of(all_ref, i, 7) for i in range(far)], join_blocks)
     q, e0, e1, c0, c1, r0, r1 = whole
     e0, e1 = e0 + 0.25 * c0, e1 + 0.25 * c1
     h = 1.0 / (q + e1)
     qh = q * h
     u0 = (r0 + qh * r1) / (e0 + qh * e1)
-    u0, u1 = chosen(ends(u0, h * r1 + qh * u0), ends_ref, me // RING_X)
-    _, ends = tree([parts_of(ring_ref, i, 7) for i in range(RING_X)], join_blocks)
-    u0, u1 = chosen(ends(u0, u1), ends_ref, me % RING_X)
+    u0, u1 = chosen(ends(u0, h * r1 + qh * u0), ends_ref, me // NEAR_X)
+    _, ends = tree([parts_of(near_ref, i, 7) for i in range(NEAR_X)], join_blocks)
+    u0, u1 = chosen(ends(u0, u1), ends_ref, me % NEAR_X)
 
     def emit(k, w):
         u_ref[rows(k), :] = w - 2.0 * f_ref[rows(k), :]
@@ -232,32 +232,24 @@
     backward(u0, u1, gr_ref, n_ref, m_ref, emit)
     r0, r1 = forward(lambda k: u_ref[turned(k), :], gy_ref, ny_ref, my_ref, gry_ref)
     kappa, ea, eb, qh, fh, h = parts_of(mat_ref, 0, 6)
-    replicate(pay_ref, (kappa, ea, eb, r0 + qh * r1, fh * r1), 1)
+    replicate(pay_ref, (kappa, ea, eb, r0 + qh * r1, fh * r1), NEAR_Y)
     hr_ref[...] = h * r1
 
 
-def core_pair(own_ref, other_ref):
-    odd = lax.axis_index("gy") % CORES == 1
-    own, other = parts_of(own_ref, 0, 5), parts_of(other_ref, 0, 5)
-    low = tuple(jnp.where(odd, b, a) for a, b in zip(own, other))
-    high = tuple(jnp.where(odd, a, b) for a, b in zip(own, other))
-    return join_elements(low, high)
-
-
-def y_merge_kernel(rings, own_ref, other_ref, pay_ref):
-    whole, _ = core_pair(own_ref, other_ref)
-    replicate(pay_ref, whole, rings)
+def y_merge_kernel(far, got_ref, pay_ref):
+    whole, _ = tree([parts_of(got_ref, i, 5) for i in range(NEAR_Y)], join_elements)
+    replicate(pay_ref, whole, far)
 
 
 def y_back_kernel(
-    rings, all_ref, own_ref, other_ref, mat_ref, hr_ref, f_ref, gry_ref, ny_ref, my_ref, low_ref, high_ref, last_ref, out_ref, u_ref, ends_ref
+    far, near_ref, all_ref, mat_ref, hr_ref, f_ref, gry_ref, ny_ref, my_ref, low_ref, high_ref, last_ref, out_ref, u_ref, ends_ref
 ):
     me = lax.axis_index("gy")
-    (kappa, ea, _, ra, _), ends = tree([parts_of(all_ref, i, 5) for i in range(rings)], join_elements)
+    (kappa, ea, _, ra, _), ends = tree([parts_of(all_ref, i, 5) for i in range(far)], join_elements)
     u0 = ra / (kappa + ea)
-    u0, u1 = chosen(ends(u0, jnp.zeros_like(u0)), ends_ref, me // CORES)
-    _, expand = core_pair(own_ref, other_ref)
-    u0, u_next = chosen(expand(u0, u1), ends_ref, me % CORES)
+    u0, u1 = chosen(ends(u0, jnp.zeros_like(u0)), ends_ref, me // NEAR_Y)
+    _, ends = tree([parts_of(near_ref, i, 5) for i in range(NEAR_Y)], join_elements)
+    u0, u_next = chosen(ends(u0, u1), ends_ref, me % NEAR_Y)
     u1 = hr_ref[...] + mat_ref[rows(3), :] * u0 + mat_ref[rows(4), :] * u_next
 
     def emit(k, u):
@@ -294,7 +286,7 @@
 
 def body(field, conductance, source):
     size_x, size_y = lax.axis_size("gx"), lax.axis_size("gy")
-    rings_x, rings_y = size_x // RING_X, size_y // CORES
+    far_x, far_y = size_x // NEAR_X, size_y // NEAR_Y
     f, c, s = (part.reshape(CELLS, LANES) for part in (field, conductance, source))
     whole, block = shape(CELLS, LANES), (CELLS, LANES)
     f, c, last, first, rhs, gx, nx, mx, mat_x = call(
@@ -310,22 +302,22 @@
         matrix_kernel, (whole, whole, whole, shape(3 * N, LANES), coefficients, coefficients, whole)
     )(c)
     grx, pay, mat_y = call(
-        x_forward_kernel, (whole, shape(RING_X * 7 * N, LANES), shape(6 * N, LANES)), [block]
+        x_forward_kernel, (whole, shape(NEAR_X * 7 * N, LANES), shape(6 * N, LANES)), [block]
     )(f, c, rhs, gx, nx, mx, mat_x, mat_y, from_down, from_up)
-    ring = gathered(pay, "gx", [[RING_X * i + j for j in range(RING_X)] for i in range(rings_x)])
-    pay = call(lambda *refs: x_merge_kernel(rings_x, *refs), shape(rings_x * 7 * N, LANES))(ring)
-    every = gathered(pay, "gx", [[RING_X * i + j for i in range(rings_x)] for j in range(RING_X)])
-    gry, own, hr = call(
-        lambda *refs: x_back_kernel(rings_x, *refs),
-        (whole, shape(5 * N, LANES), shape(N, LANES)),
-        [block, (2 * max(rings_x, RING_X) * N, LANES)],
-    )(ring, every, f, grx, nx, mx, gy, ny, my, mat_y)
-    other = lax.ppermute(own, "gy", [(i, i ^ 1) for i in range(size_y)])
-    pay = call(lambda *refs: y_merge_kernel(rings_y, *refs), shape(rings_y * 5 * N, LANES))(own, other)
-    every = gathered(pay, "gy", [[CORES * i + j for i in range(rings_y)] for j in range(CORES)])
+    near = gathered(pay, "gx", [[NEAR_X * i + j for j in range(NEAR_X)] for i in range(far_x)])
+    pay = call(lambda *refs: x_merge_kernel(far_x, *refs), shape(far_x * 7 * N, LANES))(near)
+    every = gathered(pay, "gx", [[NEAR_X * i + j for i in range(far_x)] for j in range(NEAR_X)])
+    gry, pay, hr = call(
+        lambda *refs: x_back_kernel(far_x, *refs),
+        (whole, shape(NEAR_Y * 5 * N, LANES), shape(N, LANES)),
+        [block, (2 * max(far_x, NEAR_X) * N, LANES)],
+    )(near, every, f, grx, nx, mx, gy, ny, my, mat_y)
+    near = gathered(pay, "gy", [[NEAR_Y * i + j for j in range(NEAR_Y)] for i in range(far_y)])
+    pay = call(lambda *refs: y_merge_kernel(far_y, *refs), shape(far_y * 5 * N, LANES))(near)
+    every = gathered(pay, "gy", [[NEAR_Y * i + j for i in range(far_y)] for j in range(NEAR_Y)])
     out = call(
-        lambda *refs: y_back_kernel(rings_y, *refs), whole, [block, (2 * rings_y * N, LANES)]
-    )(every, own, other, mat_y, hr, f, gry, ny, my, low, high, final)
+        lambda *refs: y_back_kernel(far_y, *refs), whole, [block, (2 * max(far_y, NEAR_Y) * N, LANES)]
+    )(near, every, mat_y, hr, f, gry, ny, my, low, high, final)
     return out.reshape(field.shape)
 
 

time: 71.7 us -> 69.3 us (0.967)
  starting transfers between devices: 12.4 us -> 10.1 us
  waiting for transfers between devices: 0.85 us -> 0.01 us
    ppermute x1 -> x0, starting transfers between devices: 2.33 us -> none  [body(): other = lax.ppermute(own, 'gy', [(i, i ^ 1) for i in range(size_y)])]
    ppermute x1 -> x0, waiting for transfers between devices: 0.85 us -> none  [body(): other = lax.ppermute(own, 'gy', [(i, i ^ 1) for i in range(size_y)])]
    all_to_all x3 -> x4, blocking collectives: 51.9 us -> 52.1 us  [gathered(): lax.all_to_all(pay.reshape(count, -1, LANES), axis, 0, 0, tiled=True, axi...]
  transfers between devices with their start and end apart: 3 -> 2, of which waited for: 1 -> 0; matrix products, arithmetic and copies ran while one was open for 0% -> 0% of each run, Pallas kernels for 4% -> 4%
where the time goes in v3:
time: 69.3 us; the launch traced here: 68.4 us
  blocking collectives  52.1 us (75%)
  starting transfers between devices  10.1 us (15%)
  Pallas kernels  5.07 us (7%)
  other arithmetic  1.06 us (2%)
    all_to_all x4, blocking collectives, gathered(): lax.all_to_all(pay.reshape(count, -1, LANES), axis, 0, 0, tiled=True, axi...  52.1 us
    ppermute x1, starting transfers between devices, body(): from_up = lax.ppermute(first, 'gy', [(b, a) for a, b in up])  5.48 us
    ppermute x1, starting transfers between devices, body(): from_down = lax.ppermute(last, 'gy', up)  4.59 us
    pallas_call x1, Pallas kernels, body(): call(matrix_kernel, (whole, whole, whole, shape(3 * N, LANES), coefficien...  2.85 us
    pallas_call x1, Pallas kernels, body(): call(lambda *refs: y_back_kernel(far_y, *refs), whole, [block, (2 * max(f...  1.5 us
  transfers between devices with their start and end apart: 2, of which 0 were waited for; matrix products, arithmetic and copies ran while one was open for 0% of the time, Pallas kernels for 4%

profile of v3, /device:TPU:1, one launch (start us, length us, event | category | flops | bytes accessed | tf_op | source)
XLA Modules:
  0.0 68.4 jit_solution(12154901133883043876)
XLA Ops:
  0.0 1.1 %pad_maximum_fusion.all_ref = f32[768,128]{1,0:T(8,128)S(1)} fusion(f32[256,128]{1,0:T(8,128)} %bitcast.22, f32[256,128]{1,0:T(8,128)} %bitcast.23, f32[256,128]{1,0:T(8,128)} %bitcast.24), kind=kLoop, calls=%fused_computation | loop fusion | flops 196608 | bytes 786432 | tf_op jit(solution)/shard_map/concatenate | solution.py:296
  1.1 0.3 shard_map.37
  1.3 4.6 %collective-permute-start = (f32[32,128]{1,0:T(8,128)S(1)}, f32[32,128]{1,0:T(8,128)S(1)}, u32[]{:S(2)}, u32[]{:S(2)}) collective-permute-start(f32[32,128]{1,0:T(8,128)S(1)} %get-tuple-element.35), channel_id=1, source_target_pairs={{0,1},{1,2},{2,3},{3,4},{4,5},{5,6},{6,7},{7,8},{8,9},{9,10},{10,1... | collective-permute-start | bytes 49160 | tf_op jit(solution)/shard_map/ppermute | solution.py:298
  5.9 5.5 %collective-permute-start.1 = (f32[32,128]{1,0:T(8,128)S(1)}, f32[32,128]{1,0:T(8,128)S(1)}, u32[]{:S(2)}, u32[]{:S(2)}) collective-permute-start(f32[32,128]{1,0:T(8,128)S(1)} %get-tuple-element.36), channel_id=1, source_target_pairs={{1,0},{2,1},{3,2},{4,3},{5,4},{6,5},{7,6},{8,7},{9,8},{10,9},{11,1... | collective-permute-start | bytes 49160 | tf_op jit(solution)/shard_map/ppermute | solution.py:299
  11.4 2.9 %shard_map.38 = (f32[256,128]{1,0:T(8,128)S(1)}, f32[256,128]{1,0:T(8,128)S(1)}, f32[256,128]{1,0:T(8,128)S(1)}, f32[48,128]{1,0:T(8,128)S(1)}, f32[1792,128]{1,...) custom-call(f32[256,128]{1,0:T(8,128)S(1)} %get-tuple-element.28.c_ref), custom_call_target="tpu_custom_call" | custom-call | tf_op jit(solution)/shard_map/pallas_call | solution.py:301
  14.3 0.0 collective-permute-done.down_ref
  14.3 0.0 collective-permute-done.1.up_ref
  14.3 0.1 shard_map.39
  14.4 11.7 %all_to_all.20 = f32[8,112,128]{2,1,0:T(8,128)S(1)} all-to-all(f32[8,112,128]{2,1,0:T(8,128)S(1)} %bitcast.20), channel_id=1, replica_groups={{0,16,32,48,64,80,96,112},{128,144,160,176,192,208,224,240},{256,272,28..., dimensions={0} | all-to-all | bytes 917504 | tf_op jit(solution)/shard_map/all_to_all | solution.py:281
  26.1 0.1 shard_map.40
  26.2 18.3 %all_to_all.21 = f32[4,112,128]{2,1,0:T(8,128)S(1)} all-to-all(f32[4,112,128]{2,1,0:T(8,128)S(1)} %bitcast.17), channel_id=1, replica_groups={{0,128,256,384},{16,144,272,400},{32,160,288,416},{48,176,304,432},{64,..., dimensions={0} | all-to-all | bytes 458752 | tf_op jit(solution)/shard_map/all_to_all | solution.py:281
  44.5 0.2 shard_map.41
  44.7 8.9 %all_to_all.22 = f32[4,80,128]{2,1,0:T(8,128)S(1)} all-to-all(f32[4,80,128]{2,1,0:T(8,128)S(1)} %bitcast.21), channel_id=1, replica_groups={{0,1,2,3},{4,5,6,7},{8,9,10,11},{12,13,14,15},{16,17,18,19},{20,21,22,2..., dimensions={0} | all-to-all | bytes 327680 | tf_op jit(solution)/shard_map/all_to_all | solution.py:281
  53.7 13.2 %all_to_all.23 = f32[4,80,128]{2,1,0:T(8,128)S(1)} all-to-all(f32[4,80,128]{2,1,0:T(8,128)S(1)} %bitcast.19), channel_id=1, replica_groups={{0,4,8,12},{1,5,9,13},{2,6,10,14},{3,7,11,15},{16,20,24,28},{17,21,25,2..., dimensions={0} | all-to-all | bytes 327680 | tf_op jit(solution)/shard_map/all_to_all | solution.py:281
  66.9 1.5 %shard_map.43 = f32[256,128]{1,0:T(8,128)} custom-call(f32[320,128]{1,0:T(8,128)S(1)} %bitcast.15, f32[320,128]{1,0:T(8,128)S(1)} %bitcast.18, f32[96,128]{1,0:T(8,128)S(1)} %get-tuple-element.42.refs_9_.refs_2_, f32[16,128]{1,0:T(8,128)S(1)} %get-tuple-element.44.refs_3_, f32[256,128]{1,0:T(8,128)S(1)} %get-tuple-element.27.f_ref.refs_2_.refs_4_, ...), custom_call_target="tpu_custom_call" | custom-call | tf_op jit(solution)/shard_map/pallas_call | solution.py:318
  (1 shorter events, 0.0 us)
Async XLA Ops:
  1.3 13.0 %collective-permute-start = (f32[32,128]{1,0:T(8,128)S(1)}, f32[32,128]{1,0:T(8,128)S(1)}, u32[]{:S(2)}, u32[]{:S(2)}) collective-permute-start(f32[32,128]{1,0:T(8,128)S(1)} %get-tuple-element.35), channel_id=1, source_target_pairs={{0,1},{1,2},{2,3},{3,4},{4,5},{5,6},{6,7},{7,8},{8,9},{9,10},{10,1... | collective-permute-start | bytes 49160 | tf_op jit(solution)/shard_map/ppermute | solution.py:298
  5.9 8.4 %collective-permute-start.1 = (f32[32,128]{1,0:T(8,128)S(1)}, f32[32,128]{1,0:T(8,128)S(1)}, u32[]{:S(2)}, u32[]{:S(2)}) collective-permute-start(f32[32,128]{1,0:T(8,128)S(1)} %get-tuple-element.36), channel_id=1, source_target_pairs={{1,0},{2,1},{3,2},{4,3},{5,4},{6,5},{7,6},{8,7},{9,8},{10,9},{11,1... | collective-permute-start | bytes 49160 | tf_op jit(solution)/shard_map/ppermute | solution.py:299

commit v4 on v3

--- a/solution.py
+++ b/solution.py
@@ -135,13 +135,15 @@
 
 
 def prepare_kernel(
-    all_ref, f_ref, c_ref, last_ref, first_ref, rhs_ref, g_ref, n_ref, m_ref, mat_ref, ay_ref
+    all_ref, f_ref, c_ref, outer_ref, inner_ref, rhs_ref, g_ref, n_ref, m_ref, mat_ref, ay_ref
 ):
+    odd = lax.axis_index("gy") % 2
     f_ref[...] = all_ref[pl.ds(0, CELLS), :]
     c_ref[...] = all_ref[pl.ds(CELLS, CELLS), :]
-    for edge_ref, y in ((first_ref, 0), (last_ref, N - 1)):
-        edge_ref[rows(0), :] = all_ref[turned(y), :]
-        edge_ref[rows(1), :] = all_ref[pl.ds(CELLS + y, N, stride=N), :]
+    for at in (0, 1):
+        first, last = (all_ref[pl.ds(CELLS * at + y, N, stride=N), :] for y in (0, N - 1))
+        outer_ref[rows(at), :] = jnp.where(odd == 1, last, first)
+        inner_ref[rows(at), :] = jnp.where(odd == 1, first, last)
     cells = [all_ref[rows(N + k), :] for k in range(N)]
     for k, part in enumerate(eliminated(cells, g_ref, n_ref, m_ref)):
         mat_ref[rows(k), :] = part
@@ -164,8 +166,11 @@
 
 
 def x_forward_kernel(
-    f_ref, c_ref, rhs_ref, g_ref, n_ref, m_ref, mat_ref, maty_ref, down_ref, up_ref, gr_ref, pay_ref, elem_ref, r_ref
+    f_ref, c_ref, rhs_ref, g_ref, n_ref, m_ref, mat_ref, maty_ref, outer_ref, inner_ref, gr_ref, pay_ref, elem_ref, r_ref, down_ref, up_ref
 ):
+    odd = lax.axis_index("gy") % 2 == 1
+    down_ref[...] = jnp.where(odd, inner_ref[...], outer_ref[...])
+    up_ref[...] = jnp.where(odd, outer_ref[...], inner_ref[...])
     r_ref[...] = rhs_ref[...]
     flux_down = 0.5 * (down_ref[rows(1), :] + c_ref[turned(0), :]) * (
         f_ref[turned(0), :] - down_ref[rows(0), :]
@@ -195,7 +200,7 @@
     cells = [c_ref[turned(k), :] for k in range(N)]
     for k, part in enumerate(eliminated(cells, g_ref, n_ref, m_ref)):
         mat_ref[rows(k), :] = part
-    size = 64
+    size = 256
     lane = lax.broadcasted_iota(jnp.int32, (size, LANES), 1)
     for start in range(0, CELLS, size):
         c = c_ref[pl.ds(start, size), :]
@@ -289,21 +294,22 @@
     far_x, far_y = size_x // NEAR_X, size_y // NEAR_Y
     f, c, s = (part.reshape(CELLS, LANES) for part in (field, conductance, source))
     whole, block = shape(CELLS, LANES), (CELLS, LANES)
-    f, c, last, first, rhs, gx, nx, mx, mat_x = call(
+    f, c, outer, inner, rhs, gx, nx, mx, mat_x = call(
         prepare_kernel,
         (whole, whole, shape(2 * N, LANES), shape(2 * N, LANES), whole, whole, whole, whole, shape(3 * N, LANES)),
         [block],
     )(jnp.concatenate([f, c, s]))
-    up = [(i, i + 1) for i in range(size_y - 1)]
-    from_down = lax.ppermute(last, "gy", up)
-    from_up = lax.ppermute(first, "gy", [(b, a) for a, b in up])
+    across = [(i, i + 1) for i in range(1, size_y - 1, 2)]
+    across += [(b, a) for a, b in across]
+    outer = lax.ppermute(outer, "gy", across)
+    inner = lax.ppermute(inner, "gy", [(i, i ^ 1) for i in range(size_y)])
     coefficients = shape(len(ROUNDS) * CELLS, LANES)
     gy, ny, my, mat_y, low, high, final = call(
         matrix_kernel, (whole, whole, whole, shape(3 * N, LANES), coefficients, coefficients, whole)
     )(c)
     grx, pay, mat_y = call(
-        x_forward_kernel, (whole, shape(NEAR_X * 7 * N, LANES), shape(6 * N, LANES)), [block]
-    )(f, c, rhs, gx, nx, mx, mat_x, mat_y, from_down, from_up)
+        x_forward_kernel, (whole, shape(NEAR_X * 7 * N, LANES), shape(6 * N, LANES)), [block, (2 * N, LANES), (2 * N, LANES)]
+    )(f, c, rhs, gx, nx, mx, mat_x, mat_y, outer, inner)
     near = gathered(pay, "gx", [[NEAR_X * i + j for j in range(NEAR_X)] for i in range(far_x)])
     pay = call(lambda *refs: x_merge_kernel(far_x, *refs), shape(far_x * 7 * N, LANES))(near)
     every = gathered(pay, "gx", [[NEAR_X * i + j for i in range(far_x)] for j in range(NEAR_X)])

time: 69.3 us -> 67.7 us (0.977)
  Pallas kernels: 5.07 us -> 4 us
    pallas_call x1, Pallas kernels: 2.85 us -> 1.78 us  [body(): call(matrix_kernel, (whole, whole, whole, shape(3 * N, LANES), coefficien...]
  transfers between devices with their start and end apart: 2 -> 2, of which waited for: 0 -> 0; matrix products, arithmetic and copies ran while one was open for 0% -> 0% of each run, Pallas kernels for 4% -> 3%
where the time goes in v4:
time: 67.7 us; the launch traced here: 66.8 us
  blocking collectives  52.2 us (77%)
  starting transfers between devices  9.45 us (14%)
  Pallas kernels  4 us (6%)
  other arithmetic  1.06 us (2%)
    all_to_all x4, blocking collectives, gathered(): lax.all_to_all(pay.reshape(count, -1, LANES), axis, 0, 0, tiled=True, axi...  52.2 us
    ppermute x1, starting transfers between devices, body(): inner = lax.ppermute(inner, 'gy', [(i, i ^ 1) for i in range(size_y)])  4.85 us
    ppermute x1, starting transfers between devices, body(): outer = lax.ppermute(outer, 'gy', across)  4.59 us
    pallas_call x1, Pallas kernels, body(): call(matrix_kernel, (whole, whole, whole, shape(3 * N, LANES), coefficien...  1.78 us
    pallas_call x1, Pallas kernels, body(): call(lambda *refs: y_back_kernel(far_y, *refs), whole, [block, (2 * max(f...  1.5 us
  transfers between devices with their start and end apart: 2, of which 0 were waited for; matrix products, arithmetic and copies ran while one was open for 0% of the time, Pallas kernels for 3%

profile of v4, /device:TPU:1, one launch (start us, length us, event | category | flops | bytes accessed | tf_op | source)
XLA Modules:
  0.0 66.8 jit_solution(11362197987573691810)
XLA Ops:
  0.0 1.1 %pad_maximum_fusion.all_ref = f32[768,128]{1,0:T(8,128)S(1)} fusion(f32[256,128]{1,0:T(8,128)} %bitcast.22, f32[256,128]{1,0:T(8,128)} %bitcast.23, f32[256,128]{1,0:T(8,128)} %bitcast.24), kind=kLoop, calls=%fused_computation | loop fusion | flops 196608 | bytes 786432 | tf_op jit(solution)/shard_map/concatenate | solution.py:301
  1.1 0.3 shard_map.37
  1.3 4.6 %collective-permute-start = (f32[32,128]{1,0:T(8,128)S(1)}, f32[32,128]{1,0:T(8,128)S(1)}, u32[]{:S(2)}, u32[]{:S(2)}) collective-permute-start(f32[32,128]{1,0:T(8,128)S(1)} %get-tuple-element.35), channel_id=1, source_target_pairs={{1,2},{3,4},{5,6},{7,8},{9,10},{11,12},{13,14},{2,1},{4,3},{6,5},{... | collective-permute-start | bytes 49160 | tf_op jit(solution)/shard_map/ppermute | solution.py:304
  5.9 4.9 %collective-permute-start.1 = (f32[32,128]{1,0:T(8,128)S(1)}, f32[32,128]{1,0:T(8,128)S(1)}, u32[]{:S(2)}, u32[]{:S(2)}) collective-permute-start(f32[32,128]{1,0:T(8,128)S(1)} %get-tuple-element.36), channel_id=1, source_target_pairs={{0,1},{1,0},{2,3},{3,2},{4,5},{5,4},{6,7},{7,6},{8,9},{9,8},{10,11... | collective-permute-start | bytes 49160 | tf_op jit(solution)/shard_map/ppermute | solution.py:305
  10.8 1.8 %shard_map.38 = (f32[256,128]{1,0:T(8,128)S(1)}, f32[256,128]{1,0:T(8,128)S(1)}, f32[256,128]{1,0:T(8,128)S(1)}, f32[48,128]{1,0:T(8,128)S(1)}, f32[1792,128]{1,...) custom-call(f32[256,128]{1,0:T(8,128)S(1)} %get-tuple-element.28.c_ref), custom_call_target="tpu_custom_call" | custom-call | tf_op jit(solution)/shard_map/pallas_call | solution.py:307
  12.6 0.0 collective-permute-done.outer_ref
  12.6 0.0 collective-permute-done.1.inner_ref
  12.6 0.1 shard_map.39
  12.7 10.9 %all_to_all.20 = f32[8,112,128]{2,1,0:T(8,128)S(1)} all-to-all(f32[8,112,128]{2,1,0:T(8,128)S(1)} %bitcast.20), channel_id=1, replica_groups={{0,16,32,48,64,80,96,112},{128,144,160,176,192,208,224,240},{256,272,28..., dimensions={0} | all-to-all | bytes 917504 | tf_op jit(solution)/shard_map/all_to_all | solution.py:286
  23.6 0.1 shard_map.40
  23.7 17.2 %all_to_all.21 = f32[4,112,128]{2,1,0:T(8,128)S(1)} all-to-all(f32[4,112,128]{2,1,0:T(8,128)S(1)} %bitcast.17), channel_id=1, replica_groups={{0,128,256,384},{16,144,272,400},{32,160,288,416},{48,176,304,432},{64,..., dimensions={0} | all-to-all | bytes 458752 | tf_op jit(solution)/shard_map/all_to_all | solution.py:286
  40.9 0.2 shard_map.41
  41.2 11.0 %all_to_all.22 = f32[4,80,128]{2,1,0:T(8,128)S(1)} all-to-all(f32[4,80,128]{2,1,0:T(8,128)S(1)} %bitcast.21), channel_id=1, replica_groups={{0,1,2,3},{4,5,6,7},{8,9,10,11},{12,13,14,15},{16,17,18,19},{20,21,22,2..., dimensions={0} | all-to-all | bytes 327680 | tf_op jit(solution)/shard_map/all_to_all | solution.py:286
  52.2 13.0 %all_to_all.23 = f32[4,80,128]{2,1,0:T(8,128)S(1)} all-to-all(f32[4,80,128]{2,1,0:T(8,128)S(1)} %bitcast.19), channel_id=1, replica_groups={{0,4,8,12},{1,5,9,13},{2,6,10,14},{3,7,11,15},{16,20,24,28},{17,21,25,2..., dimensions={0} | all-to-all | bytes 327680 | tf_op jit(solution)/shard_map/all_to_all | solution.py:286
  65.3 1.5 %shard_map.43 = f32[256,128]{1,0:T(8,128)} custom-call(f32[320,128]{1,0:T(8,128)S(1)} %bitcast.15, f32[320,128]{1,0:T(8,128)S(1)} %bitcast.18, f32[96,128]{1,0:T(8,128)S(1)} %get-tuple-element.42.refs_9_.refs_2_, f32[16,128]{1,0:T(8,128)S(1)} %get-tuple-element.44.refs_3_, f32[256,128]{1,0:T(8,128)S(1)} %get-tuple-element.27.f_ref.refs_2_.refs_4_, ...), custom_call_target="tpu_custom_call" | custom-call | tf_op jit(solution)/shard_map/pallas_call | solution.py:324
  (1 shorter events, 0.0 us)
Async XLA Ops:
  1.3 11.3 %collective-permute-start = (f32[32,128]{1,0:T(8,128)S(1)}, f32[32,128]{1,0:T(8,128)S(1)}, u32[]{:S(2)}, u32[]{:S(2)}) collective-permute-start(f32[32,128]{1,0:T(8,128)S(1)} %get-tuple-element.35), channel_id=1, source_target_pairs={{1,2},{3,4},{5,6},{7,8},{9,10},{11,12},{13,14},{2,1},{4,3},{6,5},{... | collective-permute-start | bytes 49160 | tf_op jit(solution)/shard_map/ppermute | solution.py:304
  5.9 6.7 %collective-permute-start.1 = (f32[32,128]{1,0:T(8,128)S(1)}, f32[32,128]{1,0:T(8,128)S(1)}, u32[]{:S(2)}, u32[]{:S(2)}) collective-permute-start(f32[32,128]{1,0:T(8,128)S(1)} %get-tuple-element.36), channel_id=1, source_target_pairs={{0,1},{1,0},{2,3},{3,2},{4,5},{5,4},{6,7},{7,6},{8,9},{9,8},{10,11... | collective-permute-start | bytes 49160 | tf_op jit(solution)/shard_map/ppermute | solution.py:305

commit v5 on v4

--- a/solution.py
+++ b/solution.py
@@ -8,7 +8,8 @@
 N = 16
 CELLS = N * N
 LANES = 128
-ROUNDS = (1, 2, 4, 8, 16, 32, 64)
+SEGMENTS = LANES // N
+ROUNDS = (1, 2, 4)
 NEAR_X = 8
 NEAR_Y = 4
 
@@ -134,16 +135,17 @@
             pay_ref[rows(len(values) * i + k), :] = value
 
 
-def prepare_kernel(
-    all_ref, f_ref, c_ref, outer_ref, inner_ref, rhs_ref, g_ref, n_ref, m_ref, mat_ref, ay_ref
-):
-    odd = lax.axis_index("gy") % 2
+def edges_kernel(all_ref, outer_ref, inner_ref):
+    odd = lax.axis_index("gy") % 2 == 1
+    for at in (0, 1):
+        first, last = (all_ref[pl.ds(CELLS * at + y, N, stride=N), :] for y in (0, N - 1))
+        outer_ref[rows(at), :] = jnp.where(odd, last, first)
+        inner_ref[rows(at), :] = jnp.where(odd, first, last)
+
+
+def prepare_kernel(all_ref, f_ref, c_ref, rhs_ref, g_ref, n_ref, m_ref, mat_ref, ay_ref):
     f_ref[...] = all_ref[pl.ds(0, CELLS), :]
     c_ref[...] = all_ref[pl.ds(CELLS, CELLS), :]
-    for at in (0, 1):
-        first, last = (all_ref[pl.ds(CELLS * at + y, N, stride=N), :] for y in (0, N - 1))
-        outer_ref[rows(at), :] = jnp.where(odd == 1, last, first)
-        inner_ref[rows(at), :] = jnp.where(odd == 1, first, last)
     cells = [all_ref[rows(N + k), :] for k in range(N)]
     for k, part in enumerate(eliminated(cells, g_ref, n_ref, m_ref)):
         mat_ref[rows(k), :] = part
@@ -196,25 +198,48 @@
     replicate(pay_ref, whole, far)
 
 
-def matrix_kernel(c_ref, g_ref, n_ref, m_ref, mat_ref, low_ref, high_ref, last_ref):
+def segment(value, s, up):
+    return pltpu.roll(value, N - s if up else s, 0)
+
+
+def matrix_kernel(
+    c_ref, g_ref, n_ref, m_ref, mat_ref, gz_ref, nz_ref, mz_ref, matz_ref, cz_ref
+):
     cells = [c_ref[turned(k), :] for k in range(N)]
     for k, part in enumerate(eliminated(cells, g_ref, n_ref, m_ref)):
         mat_ref[rows(k), :] = part
-    size = 256
-    lane = lax.broadcasted_iota(jnp.int32, (size, LANES), 1)
-    for start in range(0, CELLS, size):
-        c = c_ref[pl.ds(start, size), :]
-        inner = jnp.where(lane < LANES - 1, 0.25 * (c + pltpu.roll(c, LANES - 1, 1)), 0.0)
-        lower, upper = pltpu.roll(inner, 1, 1), inner
-        excess = jnp.where((lane > 0) & (lane < LANES - 1), 1.0, 1.0 + 0.25 * c)
-        for at, s in enumerate(ROUNDS):
-            g = 1.0 / (lower + upper + excess)
-            lg, ug, eg = lower * g, upper * g, excess * g
-            low_ref[pl.ds(at * CELLS + start, size), :] = lower * pltpu.roll(g, s, 1)
-            high_ref[pl.ds(at * CELLS + start, size), :] = upper * pltpu.roll(g, LANES - s, 1)
-            excess = excess + lower * pltpu.roll(eg, s, 1) + upper * pltpu.roll(eg, LANES - s, 1)
-            lower, upper = lower * pltpu.roll(lg, s, 1), upper * pltpu.roll(ug, LANES - s, 1)
-        last_ref[pl.ds(start, size), :] = 1.0 / excess
+    turn(c_ref, cz_ref)
+    cells = [cz_ref[turned(k), :] for k in range(N)]
+    q, e0, e1 = eliminated(cells, gz_ref, nz_ref, mz_ref)
+    place = lax.broadcasted_iota(jnp.int32, (N, LANES), 0) % SEGMENTS
+    inside_low, inside_high = place > 0, place < SEGMENTS - 1
+    c0, c1 = cells[0], cells[N - 1]
+    low = 0.25 * (jnp.where(inside_low, segment(c1, 1, False), 0.0) + c0)
+    high = 0.25 * (jnp.where(inside_high, segment(c0, 1, True), 0.0) + c1)
+    e0 = e0 + jnp.where(inside_low, 0.0, low)
+    e1 = e1 + jnp.where(inside_high, 0.0, high)
+    low = jnp.where(inside_low, low, 0.0)
+    high = jnp.where(inside_high, high, 0.0)
+    h = 1.0 / (q + high + e1)
+    qh, eh = q * h, e1 * h
+    lower = low * segment(qh, 1, False)
+    upper = qh * high
+    excess = e0 + q * eh + low * segment(eh, 1, False)
+    parts = [h, qh, high * h, low]
+    for s in ROUNDS:
+        g = 1.0 / (lower + upper + excess)
+        before, after = lower * segment(g, s, False), upper * segment(g, s, True)
+        parts += [before, after]
+        excess = excess + before * segment(excess, s, False) + after * segment(excess, s, True)
+        lower, upper = before * segment(lower, s, False), after * segment(upper, s, True)
+    for k, part in enumerate(parts + [1.0 / excess]):
+        matz_ref[rows(k), :] = part
+
+
+def turn(from_ref, to_ref):
+    for half in range(CELLS // LANES):
+        part = pl.ds(LANES * half, LANES)
+        to_ref[part, :] = from_ref[part, :].T
 
 
 def x_back_kernel(
@@ -247,7 +272,7 @@
 
 
 def y_back_kernel(
-    far, near_ref, all_ref, mat_ref, hr_ref, f_ref, gry_ref, ny_ref, my_ref, low_ref, high_ref, last_ref, out_ref, u_ref, ends_ref
+    far, near_ref, all_ref, mat_ref, hr_ref, f_ref, gry_ref, ny_ref, my_ref, gz_ref, nz_ref, mz_ref, matz_ref, out_ref, u_ref, ends_ref, uz_ref, grz_ref
 ):
     me = lax.axis_index("gy")
     (kappa, ea, _, ra, _), ends = tree([parts_of(all_ref, i, 5) for i in range(far)], join_elements)
@@ -257,19 +282,26 @@
     u0, u_next = chosen(ends(u0, u1), ends_ref, me % NEAR_Y)
     u1 = hr_ref[...] + mat_ref[rows(3), :] * u0 + mat_ref[rows(4), :] * u_next
 
-    def emit(k, u):
+    def emit_y(k, u):
         u_ref[turned(k), :] = u
 
-    backward(u0, u1, gry_ref, ny_ref, my_ref, emit)
-    right = u_ref[...]
+    backward(u0, u1, gry_ref, ny_ref, my_ref, emit_y)
+    turn(u_ref, uz_ref)
+    r0, r1 = forward(lambda k: uz_ref[turned(k), :], gz_ref, nz_ref, mz_ref, grz_ref)
+    h, qh, fh, low = parts_of(matz_ref, 0, 4)
+    right = r0 + qh * r1 + low * segment(h * r1, 1, False)
     for at, s in enumerate(ROUNDS):
-        part = pl.ds(at * CELLS, CELLS)
-        right = (
-            right
-            + low_ref[part, :] * pltpu.roll(right, s, 1)
-            + high_ref[part, :] * pltpu.roll(right, LANES - s, 1)
-        )
-    out_ref[...] = f_ref[...] + right * last_ref[...]
+        before, after = matz_ref[rows(4 + 2 * at), :], matz_ref[rows(5 + 2 * at), :]
+        right = right + before * segment(right, s, False) + after * segment(right, s, True)
+    u0 = right * matz_ref[rows(4 + 2 * len(ROUNDS)), :]
+    u1 = h * r1 + qh * u0 + fh * segment(u0, 1, True)
+
+    def emit_z(k, u):
+        uz_ref[turned(k), :] = u
+
+    backward(u0, u1, grz_ref, nz_ref, mz_ref, emit_z)
+    turn(uz_ref, u_ref)
+    out_ref[...] = f_ref[...] + u_ref[...]
 
 
 def call(kernel, outs, scratch=()):
@@ -294,18 +326,21 @@
     far_x, far_y = size_x // NEAR_X, size_y // NEAR_Y
     f, c, s = (part.reshape(CELLS, LANES) for part in (field, conductance, source))
     whole, block = shape(CELLS, LANES), (CELLS, LANES)
-    f, c, outer, inner, rhs, gx, nx, mx, mat_x = call(
-        prepare_kernel,
-        (whole, whole, shape(2 * N, LANES), shape(2 * N, LANES), whole, whole, whole, whole, shape(3 * N, LANES)),
-        [block],
-    )(jnp.concatenate([f, c, s]))
+    everything = jnp.concatenate([f, c, s])
+    edge = shape(2 * N, LANES)
+    outer, inner = call(edges_kernel, (edge, edge))(everything)
     across = [(i, i + 1) for i in range(1, size_y - 1, 2)]
     across += [(b, a) for a, b in across]
     outer = lax.ppermute(outer, "gy", across)
     inner = lax.ppermute(inner, "gy", [(i, i ^ 1) for i in range(size_y)])
-    coefficients = shape(len(ROUNDS) * CELLS, LANES)
-    gy, ny, my, mat_y, low, high, final = call(
-        matrix_kernel, (whole, whole, whole, shape(3 * N, LANES), coefficients, coefficients, whole)
+    f, c, rhs, gx, nx, mx, mat_x = call(
+        prepare_kernel, (whole, whole, whole, whole, whole, whole, shape(3 * N, LANES)), [block]
+    )(everything)
+    gy, ny, my, mat_y, gz, nz, mz, mat_z = call(
+        matrix_kernel,
+        (whole, whole, whole, shape(3 * N, LANES), whole, whole, whole)
+        + (shape((5 + 2 * len(ROUNDS)) * N, LANES),),
+        [block],
     )(c)
     grx, pay, mat_y = call(
         x_forward_kernel, (whole, shape(NEAR_X * 7 * N, LANES), shape(6 * N, LANES)), [block, (2 * N, LANES), (2 * N, LANES)]
@@ -322,8 +357,8 @@
     pay = call(lambda *refs: y_merge_kernel(far_y, *refs), shape(far_y * 5 * N, LANES))(near)
     every = gathered(pay, "gy", [[NEAR_Y * i + j for i in range(far_y)] for j in range(NEAR_Y)])
     out = call(
-        lambda *refs: y_back_kernel(far_y, *refs), whole, [block, (2 * max(far_y, NEAR_Y) * N, LANES)]
-    )(near, every, mat_y, hr, f, gry, ny, my, low, high, final)
+        lambda *refs: y_back_kernel(far_y, *refs), whole, [block, (2 * max(far_y, NEAR_Y) * N, LANES), block, block]
+    )(near, every, mat_y, hr, f, gry, ny, my, gz, nz, mz, mat_z)
     return out.reshape(field.shape)
 
 

time: 67.7 us -> 65.9 us (0.973)
  Pallas kernels: 4 us -> 2.12 us
    pallas_call x2 -> x3, Pallas kernels: 2.06 us -> 0.6 us  [the longest x1 0.32 us: body(): call(matrix_kernel, (whole, whole, whole, shape(3 * N, LANES), whole, who...]
  transfers between devices with their start and end apart: 2 -> 2, of which waited for: 0 -> 1; matrix products, arithmetic and copies ran while one was open for 0% -> 0% of each run, Pallas kernels for 3% -> 1%
where the time goes in v5:
time: 65.9 us; the launch traced here: 65 us
  blocking collectives  52.1 us (79%)
  starting transfers between devices  9.45 us (14%)
  Pallas kernels  2.12 us (3%)
  other arithmetic  1.06 us (2%)
    all_to_all x4, blocking collectives, gathered(): lax.all_to_all(pay.reshape(count, -1, LANES), axis, 0, 0, tiled=True, axi...  52.1 us
    ppermute x1, starting transfers between devices, body(): inner = lax.ppermute(inner, 'gy', [(i, i ^ 1) for i in range(size_y)])  4.85 us
    ppermute x1, starting transfers between devices, body(): outer = lax.ppermute(outer, 'gy', across)  4.59 us
  transfers between devices with their start and end apart: 2, of which 1 were waited for; matrix products, arithmetic and copies ran while one was open for 0% of the time, Pallas kernels for 1%

profile of v5, /device:TPU:1, one launch (start us, length us, event | category | flops | bytes accessed | tf_op | source)
XLA Modules:
  0.0 65.0 jit_solution(15821584997424580136)
XLA Ops:
  0.0 1.1 %pad_maximum_fusion.all_ref = f32[768,128]{1,0:T(8,128)S(1)} fusion(f32[256,128]{1,0:T(8,128)} %bitcast.22, f32[256,128]{1,0:T(8,128)} %bitcast.23, f32[256,128]{1,0:T(8,128)} %bitcast.24), kind=kLoop, calls=%fused_computation | loop fusion | flops 196608 | bytes 786432 | tf_op jit(solution)/shard_map/concatenate | solution.py:329
  1.1 4.6 %collective-permute-start = (f32[32,128]{1,0:T(8,128)S(1)}, f32[32,128]{1,0:T(8,128)S(1)}, u32[]{:S(2)}, u32[]{:S(2)}) collective-permute-start(f32[32,128]{1,0:T(8,128)S(1)} %get-tuple-element.36), channel_id=1, source_target_pairs={{1,2},{3,4},{5,6},{7,8},{9,10},{11,12},{13,14},{2,1},{4,3},{6,5},{... | collective-permute-start | bytes 49160 | tf_op jit(solution)/shard_map/ppermute | solution.py:334
  5.7 4.9 %collective-permute-start.1 = (f32[32,128]{1,0:T(8,128)S(1)}, f32[32,128]{1,0:T(8,128)S(1)}, u32[]{:S(2)}, u32[]{:S(2)}) collective-permute-start(f32[32,128]{1,0:T(8,128)S(1)} %get-tuple-element.37), channel_id=1, source_target_pairs={{0,1},{1,0},{2,3},{3,2},{4,5},{5,4},{6,7},{7,6},{8,9},{9,8},{10,11... | collective-permute-start | bytes 49160 | tf_op jit(solution)/shard_map/ppermute | solution.py:335
  10.6 0.3 shard_map.37
  10.8 0.3 shard_map.38
  11.1 0.0 collective-permute-done.outer_ref
  11.2 0.2 collective-permute-done.1.inner_ref
  11.4 0.1 shard_map.40
  11.5 11.3 %all_to_all.20 = f32[8,112,128]{2,1,0:T(8,128)S(1)} all-to-all(f32[8,112,128]{2,1,0:T(8,128)S(1)} %bitcast.20), channel_id=1, replica_groups={{0,16,32,48,64,80,96,112},{128,144,160,176,192,208,224,240},{256,272,28..., dimensions={0} | all-to-all | bytes 917504 | tf_op jit(solution)/shard_map/all_to_all | solution.py:318
  22.7 0.1 shard_map.41
  22.8 17.2 %all_to_all.21 = f32[4,112,128]{2,1,0:T(8,128)S(1)} all-to-all(f32[4,112,128]{2,1,0:T(8,128)S(1)} %bitcast.17), channel_id=1, replica_groups={{0,128,256,384},{16,144,272,400},{32,160,288,416},{48,176,304,432},{64,..., dimensions={0} | all-to-all | bytes 458752 | tf_op jit(solution)/shard_map/all_to_all | solution.py:318
  40.0 0.2 shard_map.42
  40.2 11.2 %all_to_all.22 = f32[4,80,128]{2,1,0:T(8,128)S(1)} all-to-all(f32[4,80,128]{2,1,0:T(8,128)S(1)} %bitcast.21), channel_id=1, replica_groups={{0,1,2,3},{4,5,6,7},{8,9,10,11},{12,13,14,15},{16,17,18,19},{20,21,22,2..., dimensions={0} | all-to-all | bytes 327680 | tf_op jit(solution)/shard_map/all_to_all | solution.py:318
  51.5 12.5 %all_to_all.23 = f32[4,80,128]{2,1,0:T(8,128)S(1)} all-to-all(f32[4,80,128]{2,1,0:T(8,128)S(1)} %bitcast.19), channel_id=1, replica_groups={{0,4,8,12},{1,5,9,13},{2,6,10,14},{3,7,11,15},{16,20,24,28},{17,21,25,2..., dimensions={0} | all-to-all | bytes 327680 | tf_op jit(solution)/shard_map/all_to_all | solution.py:318
  63.9 1.1 %shard_map.44 = f32[256,128]{1,0:T(8,128)} custom-call(f32[320,128]{1,0:T(8,128)S(1)} %bitcast.15, f32[320,128]{1,0:T(8,128)S(1)} %bitcast.18, f32[96,128]{1,0:T(8,128)S(1)} %get-tuple-element.43.refs_9_.refs_2_, f32[16,128]{1,0:T(8,128)S(1)} %get-tuple-element.45.refs_3_, f32[256,128]{1,0:T(8,128)S(1)} %get-tuple-element.28.f_ref.refs_2_.refs_4_, ...), custom_call_target="tpu_custom_call" | custom-call | tf_op jit(solution)/shard_map/pallas_call | solution.py:359
  (2 shorter events, 0.0 us)
Async XLA Ops:
  1.1 10.1 %collective-permute-start = (f32[32,128]{1,0:T(8,128)S(1)}, f32[32,128]{1,0:T(8,128)S(1)}, u32[]{:S(2)}, u32[]{:S(2)}) collective-permute-start(f32[32,128]{1,0:T(8,128)S(1)} %get-tuple-element.36), channel_id=1, source_target_pairs={{1,2},{3,4},{5,6},{7,8},{9,10},{11,12},{13,14},{2,1},{4,3},{6,5},{... | collective-permute-start | bytes 49160 | tf_op jit(solution)/shard_map/ppermute | solution.py:334
  5.7 5.7 %collective-permute-start.1 = (f32[32,128]{1,0:T(8,128)S(1)}, f32[32,128]{1,0:T(8,128)S(1)}, u32[]{:S(2)}, u32[]{:S(2)}) collective-permute-start(f32[32,128]{1,0:T(8,128)S(1)} %get-tuple-element.37), channel_id=1, source_target_pairs={{0,1},{1,0},{2,3},{3,2},{4,5},{5,4},{6,7},{7,6},{8,9},{9,8},{10,11... | collective-permute-start | bytes 49160 | tf_op jit(solution)/shard_map/ppermute | solution.py:335

commit v6 on v5

--- a/solution.py
+++ b/solution.py
@@ -11,6 +11,7 @@
 SEGMENTS = LANES // N
 ROUNDS = (1, 2, 4)
 NEAR_X = 8
+BLOCK = 7 * N + 8
 NEAR_Y = 4
 
 
@@ -22,11 +23,15 @@
     return pl.ds(k, N, stride=N)
 
 
+def row(k):
+    return pl.ds(k, 1)
+
+
 def shape(*dims):
     return jax.ShapeDtypeStruct(dims, jnp.float32)
 
 
-def eliminated(cells, g_ref, n_ref, m_ref):
+def eliminated(cells, g_ref, n_ref, m_ref, at=rows):
     one = jnp.ones_like(cells[0])
     half = [None] + [0.25 * (cells[k - 1] + cells[k]) for k in range(1, N)]
     first, excess, excess_first = half[1], one, one
@@ -34,31 +39,31 @@
         g = 1.0 / (first + half[k + 1] + excess)
         n = first * g
         m = half[k + 1] * g
-        g_ref[rows(k), :] = g
-        n_ref[rows(k), :] = n
-        m_ref[rows(k + 1), :] = m
+        g_ref[at(k), :] = g
+        n_ref[at(k), :] = n
+        m_ref[at(k + 1), :] = m
         excess_first = excess_first + n * excess
         first = m * first
         excess = one + m * excess
     return first, excess_first, excess
 
 
-def forward(right, g_ref, n_ref, m_ref, gr_ref):
+def forward(right, g_ref, n_ref, m_ref, gr_ref, at=rows):
     r0, carried = right(0), None
     for k in range(1, N):
-        carried = right(k) if carried is None else right(k) + m_ref[rows(k), :] * carried
+        carried = right(k) if carried is None else right(k) + m_ref[at(k), :] * carried
         if k < N - 1:
-            r0 = r0 + n_ref[rows(k), :] * carried
-            gr_ref[rows(k), :] = g_ref[rows(k), :] * carried
+            r0 = r0 + n_ref[at(k), :] * carried
+            gr_ref[at(k), :] = g_ref[at(k), :] * carried
     return r0, carried
 
 
-def backward(u0, u1, gr_ref, n_ref, m_ref, emit):
+def backward(u0, u1, gr_ref, n_ref, m_ref, emit, at=rows):
     emit(0, u0)
     emit(N - 1, u1)
     later = u1
     for k in range(N - 2, 0, -1):
-        later = gr_ref[rows(k), :] + n_ref[rows(k), :] * u0 + m_ref[rows(k + 1), :] * later
+        later = gr_ref[at(k), :] + n_ref[at(k), :] * u0 + m_ref[at(k + 1), :] * later
         emit(k, later)
 
 
@@ -115,14 +120,12 @@
     return parts[0], ends
 
 
-def chosen(found, scratch_ref, index):
+def chosen(found, scratch_ref, index, count=N):
     for i, (u0, u1) in enumerate(found):
-        scratch_ref[rows(2 * i), :] = u0
-        scratch_ref[rows(2 * i + 1), :] = u1
-    return (
-        scratch_ref[pl.ds(pl.multiple_of(index * 2 * N, 2 * N), N), :],
-        scratch_ref[pl.ds(pl.multiple_of(index * 2 * N, 2 * N) + N, N), :],
-    )
+        scratch_ref[pl.ds(2 * N * i, count), :] = u0
+        scratch_ref[pl.ds(2 * N * i + N, count), :] = u1
+    start = pl.multiple_of(index * 2 * N, 2 * N)
+    return scratch_ref[pl.ds(start, count), :], scratch_ref[pl.ds(start + N, count), :]
 
 
 def parts_of(ref, i, count):
@@ -135,15 +138,28 @@
             pay_ref[rows(len(values) * i + k), :] = value
 
 
-def edges_kernel(all_ref, outer_ref, inner_ref):
-    odd = lax.axis_index("gy") % 2 == 1
+def block_of(ref, i):
+    return tuple(ref[pl.ds(BLOCK * i + N * k, N), :] for k in range(7))
+
+
+def extra_of(ref, i):
+    return tuple(ref[row(BLOCK * i + 7 * N + k), :] for k in range(7))
+
+
+def replicate_blocks(pay_ref, values, extra, copies):
+    for i in range(copies):
+        for k, value in enumerate(values):
+            pay_ref[pl.ds(BLOCK * i + N * k, N), :] = value
+        for k, value in enumerate(extra + (jnp.zeros_like(extra[0]),)):
+            pay_ref[row(BLOCK * i + 7 * N + k), :] = value
+
+
+def edges_kernel(all_ref, last_ref):
     for at in (0, 1):
-        first, last = (all_ref[pl.ds(CELLS * at + y, N, stride=N), :] for y in (0, N - 1))
-        outer_ref[rows(at), :] = jnp.where(odd, last, first)
-        inner_ref[rows(at), :] = jnp.where(odd, first, last)
-
-
-def prepare_kernel(all_ref, f_ref, c_ref, rhs_ref, g_ref, n_ref, m_ref, mat_ref, ay_ref):
+        last_ref[rows(at), :] = all_ref[pl.ds(CELLS * at + N - 1, N, stride=N), :]
+
+
+def prepare_kernel(size_y, all_ref, f_ref, c_ref, rhs_ref, g_ref, n_ref, m_ref, mat_ref, ay_ref):
     f_ref[...] = all_ref[pl.ds(0, CELLS), :]
     c_ref[...] = all_ref[pl.ds(CELLS, CELLS), :]
     cells = [all_ref[rows(N + k), :] for k in range(N)]
@@ -156,7 +172,8 @@
         after = 0.5 * (c0 + c1) * (f1 - f0)
         ay_ref[turned(y), :] = after if flux is None else after - flux
         flux = after
-    ay_ref[turned(N - 1), :] = -flux
+    top = lax.axis_index("gy") == size_y - 1
+    ay_ref[turned(N - 1), :] = -flux - jnp.where(top, 0.5 * c1 * f1, 0.0)
     lane = lax.broadcasted_iota(jnp.int32, (N, LANES), 1)
     for k in range(N):
         c, f = cells[k], f_ref[rows(k), :]
@@ -168,34 +185,31 @@
 
 
 def x_forward_kernel(
-    f_ref, c_ref, rhs_ref, g_ref, n_ref, m_ref, mat_ref, maty_ref, outer_ref, inner_ref, gr_ref, pay_ref, elem_ref, r_ref, down_ref, up_ref
+    size_y, f_ref, c_ref, rhs_ref, g_ref, n_ref, m_ref, mat_ref, maty_ref, down_ref, gr_ref, pay_ref, elem_ref, gre_ref, ne_ref, me_ref, r_ref, ge_ref, flux_ref
 ):
-    odd = lax.axis_index("gy") % 2 == 1
-    down_ref[...] = jnp.where(odd, inner_ref[...], outer_ref[...])
-    up_ref[...] = jnp.where(odd, outer_ref[...], inner_ref[...])
     r_ref[...] = rhs_ref[...]
-    flux_down = 0.5 * (down_ref[rows(1), :] + c_ref[turned(0), :]) * (
-        f_ref[turned(0), :] - down_ref[rows(0), :]
-    )
-    flux_up = 0.5 * (up_ref[rows(1), :] + c_ref[turned(N - 1), :]) * (
-        up_ref[rows(0), :] - f_ref[turned(N - 1), :]
-    )
-    r_ref[turned(0), :] = r_ref[turned(0), :] - flux_down
-    r_ref[turned(N - 1), :] = r_ref[turned(N - 1), :] + flux_up
+    first, last, below = c_ref[turned(0), :], c_ref[turned(N - 1), :], down_ref[rows(1), :]
+    flux = 0.5 * (below + first) * (f_ref[turned(0), :] - down_ref[rows(0), :])
+    r_ref[turned(0), :] = r_ref[turned(0), :] - flux
+    flux_ref[...] = flux
     r0, r1 = forward(lambda k: r_ref[rows(k), :], g_ref, n_ref, m_ref, gr_ref)
-    values = [mat_ref[rows(k), :] for k in range(3)]
-    replicate(pay_ref, values + [c_ref[rows(0), :], c_ref[rows(N - 1), :], r0, r1], NEAR_X)
+    values = parts_of(mat_ref, 0, 3) + (c_ref[rows(0), :], c_ref[rows(N - 1), :], r0, r1)
+    cells = [down_ref[row(N + k), :] for k in range(N)]
+    extra = eliminated(cells, ge_ref, ne_ref, me_ref, row) + (cells[0], cells[N - 1])
+    extra += forward(lambda k: flux_ref[row(k), :], ge_ref, ne_ref, me_ref, gre_ref, row)
+    replicate_blocks(pay_ref, values, extra, NEAR_X)
     q, e0, e1 = parts_of(maty_ref, 0, 3)
-    face = 0.25 * (c_ref[turned(N - 1), :] + up_ref[rows(1), :])
-    e0 = e0 + jnp.where(lax.axis_index("gy") == 0, 0.25 * c_ref[turned(0), :], 0.0)
-    h = 1.0 / (q + face + e1)
+    e1 = e1 + jnp.where(lax.axis_index("gy") == size_y - 1, 0.25 * last, 0.0)
+    face = 0.25 * (below + first)
+    h = 1.0 / (q + face + e0)
     qh, fh = q * h, face * h
-    replicate(elem_ref, (qh * face, e0 + qh * e1, fh * e1, qh, fh, h), 1)
+    replicate(elem_ref, (qh * face, fh * e0, e1 + qh * e0, qh, fh, h), 1)
 
 
 def x_merge_kernel(far, got_ref, pay_ref):
-    whole, _ = tree([parts_of(got_ref, i, 7) for i in range(NEAR_X)], join_blocks)
-    replicate(pay_ref, whole, far)
+    whole, _ = tree([block_of(got_ref, i) for i in range(NEAR_X)], join_blocks)
+    extra, _ = tree([extra_of(got_ref, i) for i in range(NEAR_X)], join_blocks)
+    replicate_blocks(pay_ref, whole, extra, far)
 
 
 def segment(value, s, up):
@@ -242,28 +256,37 @@
         to_ref[part, :] = from_ref[part, :].T
 
 
-def x_back_kernel(
-    far, near_ref, all_ref, f_ref, gr_ref, n_ref, m_ref, gy_ref, ny_ref, my_ref, mat_ref, gry_ref, pay_ref, hr_ref, u_ref, ends_ref
-):
+def x_ends(far, near_ref, all_ref, part_of, ends_ref, count):
     me = lax.axis_index("gx")
-    whole, ends = tree([parts_of(all_ref, i, 7) for i in range(far)], join_blocks)
+    whole, ends = tree([part_of(all_ref, i) for i in range(far)], join_blocks)
     q, e0, e1, c0, c1, r0, r1 = whole
     e0, e1 = e0 + 0.25 * c0, e1 + 0.25 * c1
     h = 1.0 / (q + e1)
     qh = q * h
     u0 = (r0 + qh * r1) / (e0 + qh * e1)
-    u0, u1 = chosen(ends(u0, h * r1 + qh * u0), ends_ref, me // NEAR_X)
-    _, ends = tree([parts_of(near_ref, i, 7) for i in range(NEAR_X)], join_blocks)
-    u0, u1 = chosen(ends(u0, u1), ends_ref, me % NEAR_X)
+    u0, u1 = chosen(ends(u0, h * r1 + qh * u0), ends_ref, me // NEAR_X, count)
+    _, ends = tree([part_of(near_ref, i) for i in range(NEAR_X)], join_blocks)
+    return chosen(ends(u0, u1), ends_ref, me % NEAR_X, count)
+
+
+def x_back_kernel(
+    far, near_ref, all_ref, f_ref, gr_ref, n_ref, m_ref, gre_ref, ne_ref, me_ref, gy_ref, ny_ref, my_ref, mat_ref, gry_ref, pay_ref, hr_ref, u_ref, ends_ref, endse_ref, below_ref
+):
+    u0, u1 = x_ends(far, near_ref, all_ref, block_of, ends_ref, N)
+    v0, v1 = x_ends(far, near_ref, all_ref, extra_of, endse_ref, 1)
 
     def emit(k, w):
         u_ref[rows(k), :] = w - 2.0 * f_ref[rows(k), :]
 
+    def emit_below(k, w):
+        below_ref[row(k), :] = w
+
     backward(u0, u1, gr_ref, n_ref, m_ref, emit)
+    backward(v0, v1, gre_ref, ne_ref, me_ref, emit_below, row)
     r0, r1 = forward(lambda k: u_ref[turned(k), :], gy_ref, ny_ref, my_ref, gry_ref)
     kappa, ea, eb, qh, fh, h = parts_of(mat_ref, 0, 6)
-    replicate(pay_ref, (kappa, ea, eb, r0 + qh * r1, fh * r1), NEAR_Y)
-    hr_ref[...] = h * r1
+    replicate(pay_ref, (kappa, ea, eb, fh * r0 + below_ref[...], r1 + qh * r0), NEAR_Y)
+    hr_ref[...] = h * r0
 
 
 def y_merge_kernel(far, got_ref, pay_ref):
@@ -275,12 +298,12 @@
     far, near_ref, all_ref, mat_ref, hr_ref, f_ref, gry_ref, ny_ref, my_ref, gz_ref, nz_ref, mz_ref, matz_ref, out_ref, u_ref, ends_ref, uz_ref, grz_ref
 ):
     me = lax.axis_index("gy")
-    (kappa, ea, _, ra, _), ends = tree([parts_of(all_ref, i, 5) for i in range(far)], join_elements)
-    u0 = ra / (kappa + ea)
-    u0, u1 = chosen(ends(u0, jnp.zeros_like(u0)), ends_ref, me // NEAR_Y)
+    (kappa, _, eb, _, rb), ends = tree([parts_of(all_ref, i, 5) for i in range(far)], join_elements)
+    u1 = rb / (kappa + eb)
+    u0, u1 = chosen(ends(jnp.zeros_like(u1), u1), ends_ref, me // NEAR_Y)
     _, ends = tree([parts_of(near_ref, i, 5) for i in range(NEAR_Y)], join_elements)
-    u0, u_next = chosen(ends(u0, u1), ends_ref, me % NEAR_Y)
-    u1 = hr_ref[...] + mat_ref[rows(3), :] * u0 + mat_ref[rows(4), :] * u_next
+    below, u1 = chosen(ends(u0, u1), ends_ref, me % NEAR_Y)
+    u0 = hr_ref[...] + mat_ref[rows(3), :] * u1 + mat_ref[rows(4), :] * below
 
     def emit_y(k, u):
         u_ref[turned(k), :] = u
@@ -327,14 +350,10 @@
     f, c, s = (part.reshape(CELLS, LANES) for part in (field, conductance, source))
     whole, block = shape(CELLS, LANES), (CELLS, LANES)
     everything = jnp.concatenate([f, c, s])
-    edge = shape(2 * N, LANES)
-    outer, inner = call(edges_kernel, (edge, edge))(everything)
-    across = [(i, i + 1) for i in range(1, size_y - 1, 2)]
-    across += [(b, a) for a, b in across]
-    outer = lax.ppermute(outer, "gy", across)
-    inner = lax.ppermute(inner, "gy", [(i, i ^ 1) for i in range(size_y)])
+    last = call(edges_kernel, shape(2 * N, LANES))(everything)
+    down = lax.ppermute(last, "gy", [(i, i + 1) for i in range(size_y - 1)])
     f, c, rhs, gx, nx, mx, mat_x = call(
-        prepare_kernel, (whole, whole, whole, whole, whole, whole, shape(3 * N, LANES)), [block]
+        lambda *refs: prepare_kernel(size_y, *refs), (whole, whole, whole, whole, whole, whole, shape(3 * N, LANES)), [block]
     )(everything)
     gy, ny, my, mat_y, gz, nz, mz, mat_z = call(
         matrix_kernel,
@@ -342,17 +361,21 @@
         + (shape((5 + 2 * len(ROUNDS)) * N, LANES),),
         [block],
     )(c)
-    grx, pay, mat_y = call(
-        x_forward_kernel, (whole, shape(NEAR_X * 7 * N, LANES), shape(6 * N, LANES)), [block, (2 * N, LANES), (2 * N, LANES)]
-    )(f, c, rhs, gx, nx, mx, mat_x, mat_y, outer, inner)
+    line = shape(N, LANES)
+    grx, pay, mat_y, gre, ne, me = call(
+        lambda *refs: x_forward_kernel(size_y, *refs),
+        (whole, shape(NEAR_X * BLOCK, LANES), shape(6 * N, LANES), line, line, line),
+        [block, (N, LANES), (N, LANES)],
+    )(f, c, rhs, gx, nx, mx, mat_x, mat_y, down)
     near = gathered(pay, "gx", [[NEAR_X * i + j for j in range(NEAR_X)] for i in range(far_x)])
-    pay = call(lambda *refs: x_merge_kernel(far_x, *refs), shape(far_x * 7 * N, LANES))(near)
+    pay = call(lambda *refs: x_merge_kernel(far_x, *refs), shape(far_x * BLOCK, LANES))(near)
     every = gathered(pay, "gx", [[NEAR_X * i + j for i in range(far_x)] for j in range(NEAR_X)])
+    ends = (2 * max(far_x, NEAR_X) * N, LANES)
     gry, pay, hr = call(
         lambda *refs: x_back_kernel(far_x, *refs),
         (whole, shape(NEAR_Y * 5 * N, LANES), shape(N, LANES)),
-        [block, (2 * max(far_x, NEAR_X) * N, LANES)],
-    )(near, every, f, grx, nx, mx, gy, ny, my, mat_y)
+        [block, ends, ends, (N, LANES)],
+    )(near, every, f, grx, nx, mx, gre, ne, me, gy, ny, my, mat_y)
     near = gathered(pay, "gy", [[NEAR_Y * i + j for j in range(NEAR_Y)] for i in range(far_y)])
     pay = call(lambda *refs: y_merge_kernel(far_y, *refs), shape(far_y * 5 * N, LANES))(near)
     every = gathered(pay, "gy", [[NEAR_Y * i + j for i in range(far_y)] for j in range(NEAR_Y)])

time: 65.9 us -> 65.6 us (level)
  starting transfers between devices: 9.45 us -> 4.59 us
  waiting for transfers between devices: 0.21 us -> 3.63 us
  blocking collectives: 52.1 us -> 53.1 us
    ppermute x2 -> x1, starting transfers between devices: 9.45 us -> 4.59 us  [body(): down = lax.ppermute(last, 'gy', [(i, i + 1) for i in range(size_y - 1)])]
    ppermute x2 -> x1, waiting for transfers between devices: 0.21 us -> 3.63 us  [body(): down = lax.ppermute(last, 'gy', [(i, i + 1) for i in range(size_y - 1)])]
    all_to_all x4, blocking collectives: 52.1 us -> 53.1 us  [gathered(): lax.all_to_all(pay.reshape(count, -1, LANES), axis, 0, 0, tiled=True, axi...]
  transfers between devices with their start and end apart: 2 -> 1, of which waited for: 1 -> 1; matrix products, arithmetic and copies ran while one was open for 0% -> 0% of each run, Pallas kernels for 1% -> 1%
where the time goes in v6:
time: 65.6 us; the launch traced here: 64.8 us
  blocking collectives  53.1 us (81%)
  starting transfers between devices  4.59 us (7%)
  waiting for transfers between devices  3.63 us (6%)
  Pallas kernels  2.32 us (4%)
  other arithmetic  1.06 us (2%)
    all_to_all x4, blocking collectives, gathered(): lax.all_to_all(pay.reshape(count, -1, LANES), axis, 0, 0, tiled=True, axi...  53.1 us
    ppermute x1, starting transfers between devices, body(): down = lax.ppermute(last, 'gy', [(i, i + 1) for i in range(size_y - 1)])  4.59 us
    ppermute x1, waiting for transfers between devices, body(): down = lax.ppermute(last, 'gy', [(i, i + 1) for i in range(size_y - 1)])  3.63 us
  transfers between devices with their start and end apart: 1, of which 1 were waited for; matrix products, arithmetic and copies ran while one was open for 0% of the time, Pallas kernels for 1%

profile of v6, /device:TPU:1, one launch (start us, length us, event | category | flops | bytes accessed | tf_op | source)
XLA Modules:
  0.0 64.8 jit_solution(2939250493241447831)
XLA Ops:
  0.0 1.1 %pad_maximum_fusion.refs_0_.all_ref = f32[768,128]{1,0:T(8,128)S(1)} fusion(f32[256,128]{1,0:T(8,128)} %bitcast.22, f32[256,128]{1,0:T(8,128)} %bitcast.23, f32[256,128]{1,0:T(8,128)} %bitcast.24), kind=kLoop, calls=%fused_computation | loop fusion | flops 196608 | bytes 786432 | tf_op jit(solution)/shard_map/concatenate | solution.py:352
  1.1 4.6 %collective-permute-start = (f32[32,128]{1,0:T(8,128)S(1)}, f32[32,128]{1,0:T(8,128)S(1)}, u32[]{:S(2)}, u32[]{:S(2)}) collective-permute-start(f32[32,128]{1,0:T(8,128)S(1)} %shard_map.39), channel_id=1, source_target_pairs={{0,1},{1,2},{2,3},{3,4},{4,5},{5,6},{6,7},{7,8},{8,9},{9,10},{10,1... | collective-permute-start | bytes 49160 | tf_op jit(solution)/shard_map/ppermute | solution.py:354
  5.7 0.3 shard_map.37
  6.0 0.3 shard_map.38
  6.3 3.6 %collective-permute-done.refs_8_ = f32[32,128]{1,0:T(8,128)S(1)} collective-permute-done((f32[32,128]{1,0:T(8,128)S(1)}, f32[32,128]{1,0:T(8,128)S(1)}, u32[]{:S(2)}, u32[]{:S(2)}) %collective-permute-start) | collective-permute-done | bytes 16416 | tf_op jit(solution)/shard_map/ppermute | solution.py:354
  9.9 0.2 shard_map.40
  10.1 11.2 %all_to_all.20 = f32[8,120,128]{2,1,0:T(8,128)S(1)} all-to-all(f32[8,120,128]{2,1,0:T(8,128)S(1)} %bitcast.20), channel_id=1, replica_groups={{0,16,32,48,64,80,96,112},{128,144,160,176,192,208,224,240},{256,272,28..., dimensions={0} | all-to-all | bytes 983040 | tf_op jit(solution)/shard_map/all_to_all | solution.py:341
  21.4 0.1 shard_map.41
  21.5 19.1 %all_to_all.21 = f32[4,120,128]{2,1,0:T(8,128)S(1)} all-to-all(f32[4,120,128]{2,1,0:T(8,128)S(1)} %bitcast.17), channel_id=1, replica_groups={{0,128,256,384},{16,144,272,400},{32,160,288,416},{48,176,304,432},{64,..., dimensions={0} | all-to-all | bytes 491520 | tf_op jit(solution)/shard_map/all_to_all | solution.py:341
  40.6 0.3 shard_map.42
  40.9 8.5 %all_to_all.22 = f32[4,80,128]{2,1,0:T(8,128)S(1)} all-to-all(f32[4,80,128]{2,1,0:T(8,128)S(1)} %bitcast.21), channel_id=1, replica_groups={{0,1,2,3},{4,5,6,7},{8,9,10,11},{12,13,14,15},{16,17,18,19},{20,21,22,2..., dimensions={0} | all-to-all | bytes 327680 | tf_op jit(solution)/shard_map/all_to_all | solution.py:341
  49.4 14.3 %all_to_all.23 = f32[4,80,128]{2,1,0:T(8,128)S(1)} all-to-all(f32[4,80,128]{2,1,0:T(8,128)S(1)} %bitcast.19), channel_id=1, replica_groups={{0,4,8,12},{1,5,9,13},{2,6,10,14},{3,7,11,15},{16,20,24,28},{17,21,25,2..., dimensions={0} | all-to-all | bytes 327680 | tf_op jit(solution)/shard_map/all_to_all | solution.py:341
  63.7 1.1 %shard_map.44 = f32[256,128]{1,0:T(8,128)} custom-call(f32[320,128]{1,0:T(8,128)S(1)} %bitcast.15, f32[320,128]{1,0:T(8,128)S(1)} %bitcast.18, f32[96,128]{1,0:T(8,128)S(1)} %get-tuple-element.45.refs_12_.refs_2_, f32[16,128]{1,0:T(8,128)S(1)} %get-tuple-element.47.refs_3_, f32[256,128]{1,0:T(8,128)S(1)} %get-tuple-element.29.refs_0_.refs_2_.refs_4_, ...), custom_call_target="tpu_custom_call" | custom-call | tf_op jit(solution)/shard_map/pallas_call | solution.py:382
  (2 shorter events, 0.0 us)
Async XLA Ops:
  1.1 8.8 %collective-permute-start = (f32[32,128]{1,0:T(8,128)S(1)}, f32[32,128]{1,0:T(8,128)S(1)}, u32[]{:S(2)}, u32[]{:S(2)}) collective-permute-start(f32[32,128]{1,0:T(8,128)S(1)} %shard_map.39), channel_id=1, source_target_pairs={{0,1},{1,2},{2,3},{3,4},{4,5},{5,6},{6,7},{7,8},{8,9},{9,10},{10,1... | collective-permute-start | bytes 49160 | tf_op jit(solution)/shard_map/ppermute | solution.py:354

commit v7 on v6

--- a/solution.py
+++ b/solution.py
@@ -11,7 +11,7 @@
 SEGMENTS = LANES // N
 ROUNDS = (1, 2, 4)
 NEAR_X = 8
-BLOCK = 7 * N + 8
+BLOCK = 5 * N + 8
 NEAR_Y = 4
 
 
@@ -139,11 +139,11 @@
 
 
 def block_of(ref, i):
-    return tuple(ref[pl.ds(BLOCK * i + N * k, N), :] for k in range(7))
+    return tuple(ref[pl.ds(BLOCK * i + N * k, N), :] for k in range(5))
 
 
 def extra_of(ref, i):
-    return tuple(ref[row(BLOCK * i + 7 * N + k), :] for k in range(7))
+    return tuple(ref[row(BLOCK * i + 5 * N + k), :] for k in range(7))
 
 
 def replicate_blocks(pay_ref, values, extra, copies):
@@ -151,10 +151,11 @@
         for k, value in enumerate(values):
             pay_ref[pl.ds(BLOCK * i + N * k, N), :] = value
         for k, value in enumerate(extra + (jnp.zeros_like(extra[0]),)):
-            pay_ref[row(BLOCK * i + 7 * N + k), :] = value
-
-
-def edges_kernel(all_ref, last_ref):
+            pay_ref[row(BLOCK * i + 5 * N + k), :] = value
+
+
+def edges_kernel(all_ref, last_ref, front_ref):
+    front_ref[...] = all_ref[rows(N), :]
     for at in (0, 1):
         last_ref[rows(at), :] = all_ref[pl.ds(CELLS * at + N - 1, N, stride=N), :]
 
@@ -185,7 +186,7 @@
 
 
 def x_forward_kernel(
-    size_y, f_ref, c_ref, rhs_ref, g_ref, n_ref, m_ref, mat_ref, maty_ref, down_ref, gr_ref, pay_ref, elem_ref, gre_ref, ne_ref, me_ref, r_ref, ge_ref, flux_ref
+    size_y, f_ref, c_ref, rhs_ref, g_ref, n_ref, m_ref, mat_ref, maty_ref, down_ref, next_ref, gr_ref, pay_ref, elem_ref, elemx_ref, gre_ref, ne_ref, me_ref, r_ref, ge_ref, flux_ref
 ):
     r_ref[...] = rhs_ref[...]
     first, last, below = c_ref[turned(0), :], c_ref[turned(N - 1), :], down_ref[rows(1), :]
@@ -193,7 +194,13 @@
     r_ref[turned(0), :] = r_ref[turned(0), :] - flux
     flux_ref[...] = flux
     r0, r1 = forward(lambda k: r_ref[rows(k), :], g_ref, n_ref, m_ref, gr_ref)
-    values = parts_of(mat_ref, 0, 3) + (c_ref[rows(0), :], c_ref[rows(N - 1), :], r0, r1)
+    q, e0, e1 = parts_of(mat_ref, 0, 3)
+    e0 = e0 + jnp.where(lax.axis_index("gx") == 0, 0.25 * c_ref[rows(0), :], 0.0)
+    face = 0.25 * (c_ref[rows(N - 1), :] + next_ref[...])
+    h = 1.0 / (q + face + e1)
+    qh, fh = q * h, face * h
+    values = (qh * face, e0 + qh * e1, fh * e1, r0 + qh * r1, fh * r1)
+    replicate(elemx_ref, (qh, fh, h * r1), 1)
     cells = [down_ref[row(N + k), :] for k in range(N)]
     extra = eliminated(cells, ge_ref, ne_ref, me_ref, row) + (cells[0], cells[N - 1])
     extra += forward(lambda k: flux_ref[row(k), :], ge_ref, ne_ref, me_ref, gre_ref, row)
@@ -207,7 +214,7 @@
 
 
 def x_merge_kernel(far, got_ref, pay_ref):
-    whole, _ = tree([block_of(got_ref, i) for i in range(NEAR_X)], join_blocks)
+    whole, _ = tree([block_of(got_ref, i) for i in range(NEAR_X)], join_elements)
     extra, _ = tree([extra_of(got_ref, i) for i in range(NEAR_X)], join_blocks)
     replicate_blocks(pay_ref, whole, extra, far)
 
@@ -269,10 +276,21 @@
     return chosen(ends(u0, u1), ends_ref, me % NEAR_X, count)
 
 
+def x_element_ends(far, near_ref, all_ref, ends_ref):
+    me = lax.axis_index("gx")
+    (kappa, ea, _, ra, _), ends = tree([block_of(all_ref, i) for i in range(far)], join_elements)
+    u0 = ra / (kappa + ea)
+    u0, u1 = chosen(ends(u0, jnp.zeros_like(u0)), ends_ref, me // NEAR_X)
+    _, ends = tree([block_of(near_ref, i) for i in range(NEAR_X)], join_elements)
+    return chosen(ends(u0, u1), ends_ref, me % NEAR_X)
+
+
 def x_back_kernel(
-    far, near_ref, all_ref, f_ref, gr_ref, n_ref, m_ref, gre_ref, ne_ref, me_ref, gy_ref, ny_ref, my_ref, mat_ref, gry_ref, pay_ref, hr_ref, u_ref, ends_ref, endse_ref, below_ref
+    far, near_ref, all_ref, elemx_ref, f_ref, gr_ref, n_ref, m_ref, gre_ref, ne_ref, me_ref, gy_ref, ny_ref, my_ref, mat_ref, gry_ref, pay_ref, hr_ref, u_ref, ends_ref, endse_ref, below_ref
 ):
-    u0, u1 = x_ends(far, near_ref, all_ref, block_of, ends_ref, N)
+    u0, u_next = x_element_ends(far, near_ref, all_ref, ends_ref)
+    qh, fh, hr = parts_of(elemx_ref, 0, 3)
+    u1 = hr + qh * u0 + fh * u_next
     v0, v1 = x_ends(far, near_ref, all_ref, extra_of, endse_ref, 1)
 
     def emit(k, w):
@@ -350,8 +368,9 @@
     f, c, s = (part.reshape(CELLS, LANES) for part in (field, conductance, source))
     whole, block = shape(CELLS, LANES), (CELLS, LANES)
     everything = jnp.concatenate([f, c, s])
-    last = call(edges_kernel, shape(2 * N, LANES))(everything)
+    last, front = call(edges_kernel, (shape(2 * N, LANES), shape(N, LANES)))(everything)
     down = lax.ppermute(last, "gy", [(i, i + 1) for i in range(size_y - 1)])
+    following = lax.ppermute(front, "gx", [(i + 1, i) for i in range(size_x - 1)])
     f, c, rhs, gx, nx, mx, mat_x = call(
         lambda *refs: prepare_kernel(size_y, *refs), (whole, whole, whole, whole, whole, whole, shape(3 * N, LANES)), [block]
     )(everything)
@@ -362,11 +381,11 @@
         [block],
     )(c)
     line = shape(N, LANES)
-    grx, pay, mat_y, gre, ne, me = call(
+    grx, pay, mat_y, elem_x, gre, ne, me = call(
         lambda *refs: x_forward_kernel(size_y, *refs),
-        (whole, shape(NEAR_X * BLOCK, LANES), shape(6 * N, LANES), line, line, line),
+        (whole, shape(NEAR_X * BLOCK, LANES), shape(6 * N, LANES), shape(3 * N, LANES), line, line, line),
         [block, (N, LANES), (N, LANES)],
-    )(f, c, rhs, gx, nx, mx, mat_x, mat_y, down)
+    )(f, c, rhs, gx, nx, mx, mat_x, mat_y, down, following)
     near = gathered(pay, "gx", [[NEAR_X * i + j for j in range(NEAR_X)] for i in range(far_x)])
     pay = call(lambda *refs: x_merge_kernel(far_x, *refs), shape(far_x * BLOCK, LANES))(near)
     every = gathered(pay, "gx", [[NEAR_X * i + j for i in range(far_x)] for j in range(NEAR_X)])
@@ -375,7 +394,7 @@
         lambda *refs: x_back_kernel(far_x, *refs),
         (whole, shape(NEAR_Y * 5 * N, LANES), shape(N, LANES)),
         [block, ends, ends, (N, LANES)],
-    )(near, every, f, grx, nx, mx, gre, ne, me, gy, ny, my, mat_y)
+    )(near, every, elem_x, f, grx, nx, mx, gre, ne, me, gy, ny, my, mat_y)
     near = gathered(pay, "gy", [[NEAR_Y * i + j for j in range(NEAR_Y)] for i in range(far_y)])
     pay = call(lambda *refs: y_merge_kernel(far_y, *refs), shape(far_y * 5 * N, LANES))(near)
     every = gathered(pay, "gy", [[NEAR_Y * i + j for i in range(far_y)] for j in range(NEAR_Y)])

time: 65.6 us -> 67.8 us (1.034)
  blocking collectives: 53.1 us -> 55.1 us
  starting transfers between devices: 4.59 us -> 5.89 us
  waiting for transfers between devices: 3.63 us -> 2.5 us
    ppermute x1, waiting for transfers between devices: 3.63 us -> 0.01 us  [body(): down = lax.ppermute(last, 'gy', [(i, i + 1) for i in range(size_y - 1)])]
    ppermute x0 -> x1, waiting for transfers between devices: none -> 2.5 us  [body(): lax.ppermute(front, 'gx', [(i + 1, i) for i in range(size_x - 1)])]
    all_to_all x4, blocking collectives: 53.1 us -> 55.1 us  [gathered(): lax.all_to_all(pay.reshape(count, -1, LANES), axis, 0, 0, tiled=True, axi...]
    ppermute x0 -> x1, starting transfers between devices: none -> 1.29 us  [body(): lax.ppermute(front, 'gx', [(i + 1, i) for i in range(size_x - 1)])]
  transfers between devices with their start and end apart: 1 -> 2, of which waited for: 1 -> 1; matrix products, arithmetic and copies ran while one was open for 0% -> 0% of each run, Pallas kernels for 1% -> 1%
where the time goes in v7:
time: 67.8 us; the launch traced here: 66.9 us
  blocking collectives  55.1 us (81%)
  starting transfers between devices  5.89 us (9%)
  waiting for transfers between devices  2.5 us (4%)
  Pallas kernels  2.25 us (3%)
  other arithmetic  1.06 us (2%)
    all_to_all x4, blocking collectives, gathered(): lax.all_to_all(pay.reshape(count, -1, LANES), axis, 0, 0, tiled=True, axi...  55.1 us
    ppermute x1, starting transfers between devices, body(): down = lax.ppermute(last, 'gy', [(i, i + 1) for i in range(size_y - 1)])  4.59 us
    ppermute x1, waiting for transfers between devices, body(): lax.ppermute(front, 'gx', [(i + 1, i) for i in range(size_x - 1)])  2.5 us
  transfers between devices with their start and end apart: 2, of which 1 were waited for; matrix products, arithmetic and copies ran while one was open for 0% of the time, Pallas kernels for 1%

profile of v7, /device:TPU:1, one launch (start us, length us, event | category | flops | bytes accessed | tf_op | source)
XLA Modules:
  0.0 66.9 jit_solution(10409294607021471063)
XLA Ops:
  0.0 1.1 %pad_maximum_fusion.refs_0_.all_ref = f32[768,128]{1,0:T(8,128)S(1)} fusion(f32[256,128]{1,0:T(8,128)} %bitcast.22, f32[256,128]{1,0:T(8,128)} %bitcast.23, f32[256,128]{1,0:T(8,128)} %bitcast.24), kind=kLoop, calls=%fused_computation | loop fusion | flops 196608 | bytes 786432 | tf_op jit(solution)/shard_map/concatenate | solution.py:370
  1.1 4.6 %collective-permute-start = (f32[32,128]{1,0:T(8,128)S(1)}, f32[32,128]{1,0:T(8,128)S(1)}, u32[]{:S(2)}, u32[]{:S(2)}) collective-permute-start(f32[32,128]{1,0:T(8,128)S(1)} %get-tuple-element.40), channel_id=1, source_target_pairs={{0,1},{1,2},{2,3},{3,4},{4,5},{5,6},{6,7},{7,8},{8,9},{9,10},{10,1... | collective-permute-start | bytes 49160 | tf_op jit(solution)/shard_map/ppermute | solution.py:372
  5.7 1.3 %collective-permute-start.1 = (f32[16,128]{1,0:T(8,128)S(1)}, f32[16,128]{1,0:T(8,128)S(1)}, u32[]{:S(2)}, u32[]{:S(2)}) collective-permute-start(f32[16,128]{1,0:T(8,128)S(1)} %get-tuple-element.41), channel_id=1, source_target_pairs={{16,0},{32,16},{48,32},{64,48},{80,64},{96,80},{112,96},{128,112},... | collective-permute-start | bytes 24584 | tf_op jit(solution)/shard_map/ppermute | solution.py:373
  7.0 0.3 shard_map.37
  7.3 0.3 shard_map.38
  7.6 2.5 %collective-permute-done.1.refs_9_ = f32[16,128]{1,0:T(8,128)S(1)} collective-permute-done((f32[16,128]{1,0:T(8,128)S(1)}, f32[16,128]{1,0:T(8,128)S(1)}, u32[]{:S(2)}, u32[]{:S(2)}) %collective-permute-start.1) | collective-permute-done | bytes 8224 | tf_op jit(solution)/shard_map/ppermute | solution.py:373
  10.1 0.0 collective-permute-done.refs_8_
  10.1 0.2 shard_map.40
  10.3 15.4 %all_to_all.20 = f32[8,88,128]{2,1,0:T(8,128)S(1)} all-to-all(f32[8,88,128]{2,1,0:T(8,128)S(1)} %bitcast.20), channel_id=1, replica_groups={{0,16,32,48,64,80,96,112},{128,144,160,176,192,208,224,240},{256,272,28..., dimensions={0} | all-to-all | bytes 720896 | tf_op jit(solution)/shard_map/all_to_all | solution.py:359
  25.7 0.1 shard_map.41
  25.8 16.4 %all_to_all.21 = f32[4,88,128]{2,1,0:T(8,128)S(1)} all-to-all(f32[4,88,128]{2,1,0:T(8,128)S(1)} %bitcast.17), channel_id=1, replica_groups={{0,128,256,384},{16,144,272,400},{32,160,288,416},{48,176,304,432},{64,..., dimensions={0} | all-to-all | bytes 360448 | tf_op jit(solution)/shard_map/all_to_all | solution.py:359
  42.2 0.2 shard_map.42
  42.4 10.7 %all_to_all.22 = f32[4,80,128]{2,1,0:T(8,128)S(1)} all-to-all(f32[4,80,128]{2,1,0:T(8,128)S(1)} %bitcast.21), channel_id=1, replica_groups={{0,1,2,3},{4,5,6,7},{8,9,10,11},{12,13,14,15},{16,17,18,19},{20,21,22,2..., dimensions={0} | all-to-all | bytes 327680 | tf_op jit(solution)/shard_map/all_to_all | solution.py:359
  53.2 12.6 %all_to_all.23 = f32[4,80,128]{2,1,0:T(8,128)S(1)} all-to-all(f32[4,80,128]{2,1,0:T(8,128)S(1)} %bitcast.19), channel_id=1, replica_groups={{0,4,8,12},{1,5,9,13},{2,6,10,14},{3,7,11,15},{16,20,24,28},{17,21,25,2..., dimensions={0} | all-to-all | bytes 327680 | tf_op jit(solution)/shard_map/all_to_all | solution.py:359
  65.8 1.1 %shard_map.44 = f32[256,128]{1,0:T(8,128)} custom-call(f32[320,128]{1,0:T(8,128)S(1)} %bitcast.15, f32[320,128]{1,0:T(8,128)S(1)} %bitcast.18, f32[96,128]{1,0:T(8,128)S(1)} %get-tuple-element.51.refs_13_.refs_2_, f32[16,128]{1,0:T(8,128)S(1)} %get-tuple-element.53.refs_3_, f32[256,128]{1,0:T(8,128)S(1)} %get-tuple-element.32.refs_0_.refs_3_.refs_4_, ...), custom_call_target="tpu_custom_call" | custom-call | tf_op jit(solution)/shard_map/pallas_call | solution.py:401
  (2 shorter events, 0.0 us)
Async XLA Ops:
  1.1 9.0 %collective-permute-start = (f32[32,128]{1,0:T(8,128)S(1)}, f32[32,128]{1,0:T(8,128)S(1)}, u32[]{:S(2)}, u32[]{:S(2)}) collective-permute-start(f32[32,128]{1,0:T(8,128)S(1)} %get-tuple-element.40), channel_id=1, source_target_pairs={{0,1},{1,2},{2,3},{3,4},{4,5},{5,6},{6,7},{7,8},{8,9},{9,10},{10,1... | collective-permute-start | bytes 49160 | tf_op jit(solution)/shard_map/ppermute | solution.py:372
  5.7 4.4 %collective-permute-start.1 = (f32[16,128]{1,0:T(8,128)S(1)}, f32[16,128]{1,0:T(8,128)S(1)}, u32[]{:S(2)}, u32[]{:S(2)}) collective-permute-start(f32[16,128]{1,0:T(8,128)S(1)} %get-tuple-element.41), channel_id=1, source_target_pairs={{16,0},{32,16},{48,32},{64,48},{80,64},{96,80},{112,96},{128,112},... | collective-permute-start | bytes 24584 | tf_op jit(solution)/shard_map/ppermute | solution.py:373

commit v8 on v6

--- a/solution.py
+++ b/solution.py
@@ -159,7 +159,7 @@
         last_ref[rows(at), :] = all_ref[pl.ds(CELLS * at + N - 1, N, stride=N), :]
 
 
-def prepare_kernel(size_y, all_ref, f_ref, c_ref, rhs_ref, g_ref, n_ref, m_ref, mat_ref, ay_ref):
+def prepare_kernel(size_y, all_ref, s_ref, f_ref, c_ref, rhs_ref, g_ref, n_ref, m_ref, mat_ref, ay_ref):
     f_ref[...] = all_ref[pl.ds(0, CELLS), :]
     c_ref[...] = all_ref[pl.ds(CELLS, CELLS), :]
     cells = [all_ref[rows(N + k), :] for k in range(N)]
@@ -181,7 +181,7 @@
         f_next = jnp.where(lane < LANES - 1, pltpu.roll(f, LANES - 1, 1), 0.0)
         upper = 0.5 * (c + c_next) * (f_next - f)
         lower = jnp.where(lane > 0, pltpu.roll(upper, 1, 1), 0.5 * c * f)
-        rhs_ref[rows(k), :] = 2.0 * f + all_ref[rows(2 * N + k), :] + ay_ref[rows(k), :] + (upper - lower)
+        rhs_ref[rows(k), :] = 2.0 * f + s_ref[rows(k), :] + ay_ref[rows(k), :] + (upper - lower)
 
 
 def x_forward_kernel(
@@ -295,7 +295,7 @@
 
 
 def y_back_kernel(
-    far, near_ref, all_ref, mat_ref, hr_ref, f_ref, gry_ref, ny_ref, my_ref, gz_ref, nz_ref, mz_ref, matz_ref, out_ref, u_ref, ends_ref, uz_ref, grz_ref
+    far, near_ref, all_ref, mat_ref, hr_ref, f_ref, gry_ref, ny_ref, my_ref, gz_ref, nz_ref, mz_ref, matz_ref, out_ref, u_ref, ends_ref, uz_ref, grz_ref, done_ref, sem
 ):
     me = lax.axis_index("gy")
     (kappa, _, eb, _, rb), ends = tree([parts_of(all_ref, i, 5) for i in range(far)], join_elements)
@@ -323,16 +323,27 @@
         uz_ref[turned(k), :] = u
 
     backward(u0, u1, grz_ref, nz_ref, mz_ref, emit_z)
-    turn(uz_ref, u_ref)
-    out_ref[...] = f_ref[...] + u_ref[...]
-
-
-def call(kernel, outs, scratch=()):
+    copies = []
+    for half in range(CELLS // LANES):
+        part = pl.ds(LANES * half, LANES)
+        done_ref[part, :] = f_ref[part, :] + uz_ref[part, :].T
+        copies.append(
+            pltpu.make_async_copy(done_ref.at[part, :], out_ref.at[part, :], sem.at[half])
+        )
+        copies[half].start()
+    for copy in copies:
+        copy.wait()
+
+
+def call(kernel, outs, scratch=(), **kwargs):
     return pl.pallas_call(
         kernel,
         out_shape=outs,
-        scratch_shapes=[pltpu.VMEM(part, jnp.float32) for part in scratch],
+        scratch_shapes=[
+            pltpu.VMEM(part, jnp.float32) if isinstance(part, tuple) else part for part in scratch
+        ],
         compiler_params=pltpu.CompilerParams(vmem_limit_bytes=16 * 1024 * 1024),
+        **kwargs,
     )
 
 
@@ -349,12 +360,12 @@
     far_x, far_y = size_x // NEAR_X, size_y // NEAR_Y
     f, c, s = (part.reshape(CELLS, LANES) for part in (field, conductance, source))
     whole, block = shape(CELLS, LANES), (CELLS, LANES)
-    everything = jnp.concatenate([f, c, s])
+    everything = jnp.concatenate([f, c])
     last = call(edges_kernel, shape(2 * N, LANES))(everything)
     down = lax.ppermute(last, "gy", [(i, i + 1) for i in range(size_y - 1)])
     f, c, rhs, gx, nx, mx, mat_x = call(
         lambda *refs: prepare_kernel(size_y, *refs), (whole, whole, whole, whole, whole, whole, shape(3 * N, LANES)), [block]
-    )(everything)
+    )(everything, s)
     gy, ny, my, mat_y, gz, nz, mz, mat_z = call(
         matrix_kernel,
         (whole, whole, whole, shape(3 * N, LANES), whole, whole, whole)
@@ -380,7 +391,9 @@
     pay = call(lambda *refs: y_merge_kernel(far_y, *refs), shape(far_y * 5 * N, LANES))(near)
     every = gathered(pay, "gy", [[NEAR_Y * i + j for i in range(far_y)] for j in range(NEAR_Y)])
     out = call(
-        lambda *refs: y_back_kernel(far_y, *refs), whole, [block, (2 * max(far_y, NEAR_Y) * N, LANES), block, block]
+        lambda *refs: y_back_kernel(far_y, *refs), whole,
+        [block, (2 * max(far_y, NEAR_Y) * N, LANES), block, block, block, pltpu.SemaphoreType.DMA((2,))],
+        out_specs=pl.BlockSpec(memory_space=pl.ANY),
     )(near, every, mat_y, hr, f, gry, ny, my, gz, nz, mz, mat_z)
     return out.reshape(field.shape)
 

time: 65.6 us -> 65.7 us (level)
  no operation moved by 1% of the time
where the time goes in v8:
time: 65.7 us; the launch traced here: 64.9 us
  blocking collectives  53.1 us (81%)
  starting transfers between devices  4.73 us (7%)
  waiting for transfers between devices  3.63 us (6%)
  Pallas kernels  2.32 us (4%)
  other arithmetic  0.99 us (2%)
    all_to_all x4, blocking collectives, gathered(): lax.all_to_all(pay.reshape(count, -1, LANES), axis, 0, 0, tiled=True, axi...  53.1 us
    ppermute x1, starting transfers between devices, body(): down = lax.ppermute(last, 'gy', [(i, i + 1) for i in range(size_y - 1)])  4.73 us
    ppermute x1, waiting for transfers between devices, body(): down = lax.ppermute(last, 'gy', [(i, i + 1) for i in range(size_y - 1)])  3.63 us
  transfers between devices with their start and end apart: 1, of which 1 were waited for; matrix products, arithmetic and copies ran while one was open for 0% of the time, Pallas kernels for 1%

profile of v8, /device:TPU:1, one launch (start us, length us, event | category | flops | bytes accessed | tf_op | source)
XLA Modules:
  0.0 64.9 jit_solution(17638981139625963160)
XLA Ops:
  0.0 1.0 %pad_maximum_fusion.refs_0_.all_ref = f32[512,128]{1,0:T(8,128)S(1)} fusion(f32[256,128]{1,0:T(8,128)} %bitcast.23, f32[256,128]{1,0:T(8,128)} %bitcast.24), kind=kLoop, calls=%fused_computation | loop fusion | flops 65536 | bytes 524288 | tf_op jit(solution)/shard_map/concatenate | solution.py:363
  1.0 0.0 copy-start
  1.0 4.7 %collective-permute-start = (f32[32,128]{1,0:T(8,128)S(1)}, f32[32,128]{1,0:T(8,128)S(1)}, u32[]{:S(2)}, u32[]{:S(2)}) collective-permute-start(f32[32,128]{1,0:T(8,128)S(1)} %shard_map.39), channel_id=1, source_target_pairs={{0,1},{1,2},{2,3},{3,4},{4,5},{5,6},{6,7},{7,8},{8,9},{9,10},{10,1... | collective-permute-start | bytes 49160 | tf_op jit(solution)/shard_map/ppermute | solution.py:365
  5.8 0.0 copy-done
  5.8 0.3 shard_map.37
  6.0 0.3 shard_map.38
  6.4 3.6 %collective-permute-done.refs_8_ = f32[32,128]{1,0:T(8,128)S(1)} collective-permute-done((f32[32,128]{1,0:T(8,128)S(1)}, f32[32,128]{1,0:T(8,128)S(1)}, u32[]{:S(2)}, u32[]{:S(2)}) %collective-permute-start) | collective-permute-done | bytes 16416 | tf_op jit(solution)/shard_map/ppermute | solution.py:365
  10.0 0.2 shard_map.40
  10.2 11.2 %all_to_all.20 = f32[8,120,128]{2,1,0:T(8,128)S(1)} all-to-all(f32[8,120,128]{2,1,0:T(8,128)S(1)} %bitcast.20), channel_id=1, replica_groups={{0,16,32,48,64,80,96,112},{128,144,160,176,192,208,224,240},{256,272,28..., dimensions={0} | all-to-all | bytes 983040 | tf_op jit(solution)/shard_map/all_to_all | solution.py:352
  21.4 0.1 shard_map.41
  21.6 19.1 %all_to_all.21 = f32[4,120,128]{2,1,0:T(8,128)S(1)} all-to-all(f32[4,120,128]{2,1,0:T(8,128)S(1)} %bitcast.17), channel_id=1, replica_groups={{0,128,256,384},{16,144,272,400},{32,160,288,416},{48,176,304,432},{64,..., dimensions={0} | all-to-all | bytes 491520 | tf_op jit(solution)/shard_map/all_to_all | solution.py:352
  40.7 0.3 shard_map.42
  41.0 8.5 %all_to_all.22 = f32[4,80,128]{2,1,0:T(8,128)S(1)} all-to-all(f32[4,80,128]{2,1,0:T(8,128)S(1)} %bitcast.21), channel_id=1, replica_groups={{0,1,2,3},{4,5,6,7},{8,9,10,11},{12,13,14,15},{16,17,18,19},{20,21,22,2..., dimensions={0} | all-to-all | bytes 327680 | tf_op jit(solution)/shard_map/all_to_all | solution.py:352
  49.5 14.3 %all_to_all.23 = f32[4,80,128]{2,1,0:T(8,128)S(1)} all-to-all(f32[4,80,128]{2,1,0:T(8,128)S(1)} %bitcast.19), channel_id=1, replica_groups={{0,4,8,12},{1,5,9,13},{2,6,10,14},{3,7,11,15},{16,20,24,28},{17,21,25,2..., dimensions={0} | all-to-all | bytes 327680 | tf_op jit(solution)/shard_map/all_to_all | solution.py:352
  63.8 1.1 %shard_map.44 = f32[256,128]{1,0:T(8,128)} custom-call(f32[320,128]{1,0:T(8,128)S(1)} %bitcast.15, f32[320,128]{1,0:T(8,128)S(1)} %bitcast.18, f32[96,128]{1,0:T(8,128)S(1)} %get-tuple-element.45.refs_12_.refs_2_, f32[16,128]{1,0:T(8,128)S(1)} %get-tuple-element.47.refs_3_, f32[256,128]{1,0:T(8,128)S(1)} %get-tuple-element.29.refs_0_.refs_2_.refs_4_, ...), custom_call_target="tpu_custom_call" | custom-call | tf_op jit(solution)/shard_map/pallas_call | solution.py:393
  (2 shorter events, 0.0 us)
Async XLA Ops:
  1.0 4.8 %copy-start = (f32[16,16,128]{2,1,0:T(8,128)S(1)}, f32[16,16,128]{2,1,0:T(8,128)}, u32[]{:S(2)}) copy-start(f32[16,16,128]{2,1,0:T(8,128)} %param.5) | copy-start | bytes 393220
  1.0 9.0 %collective-permute-start = (f32[32,128]{1,0:T(8,128)S(1)}, f32[32,128]{1,0:T(8,128)S(1)}, u32[]{:S(2)}, u32[]{:S(2)}) collective-permute-start(f32[32,128]{1,0:T(8,128)S(1)} %shard_map.39), channel_id=1, source_target_pairs={{0,1},{1,2},{2,3},{3,4},{4,5},{5,6},{6,7},{7,8},{8,9},{9,10},{10,1... | collective-permute-start | bytes 49160 | tf_op jit(solution)/shard_map/ppermute | solution.py:365

commit v9 on v8

--- a/solution.py
+++ b/solution.py
@@ -250,6 +250,12 @@
         matz_ref[rows(k), :] = part
 
 
+def setup_kernel(size_y, all_ref, s_ref, *refs):
+    prepared, matrices, (ay_ref, cz_ref) = refs[:7], refs[7:15], refs[15:]
+    prepare_kernel(size_y, all_ref, s_ref, *prepared, ay_ref)
+    matrix_kernel(prepared[1], *matrices, cz_ref)
+
+
 def turn(from_ref, to_ref):
     for half in range(CELLS // LANES):
         part = pl.ds(LANES * half, LANES)
@@ -363,15 +369,13 @@
     everything = jnp.concatenate([f, c])
     last = call(edges_kernel, shape(2 * N, LANES))(everything)
     down = lax.ppermute(last, "gy", [(i, i + 1) for i in range(size_y - 1)])
-    f, c, rhs, gx, nx, mx, mat_x = call(
-        lambda *refs: prepare_kernel(size_y, *refs), (whole, whole, whole, whole, whole, whole, shape(3 * N, LANES)), [block]
+    f, c, rhs, gx, nx, mx, mat_x, gy, ny, my, mat_y, gz, nz, mz, mat_z = call(
+        lambda *refs: setup_kernel(size_y, *refs),
+        (whole, whole, whole, whole, whole, whole, shape(3 * N, LANES))
+        + (whole, whole, whole, shape(3 * N, LANES), whole, whole, whole)
+        + (shape((5 + 2 * len(ROUNDS)) * N, LANES),),
+        [block, block],
     )(everything, s)
-    gy, ny, my, mat_y, gz, nz, mz, mat_z = call(
-        matrix_kernel,
-        (whole, whole, whole, shape(3 * N, LANES), whole, whole, whole)
-        + (shape((5 + 2 * len(ROUNDS)) * N, LANES),),
-        [block],
-    )(c)
     line = shape(N, LANES)
     grx, pay, mat_y, gre, ne, me = call(
         lambda *refs: x_forward_kernel(size_y, *refs),

time: 65.7 us -> 65.7 us (level)
  no operation moved by 1% of the time
where the time goes in v9:
time: 65.7 us; the launch traced here: 64.9 us
  blocking collectives  53.1 us (81%)
  starting transfers between devices  4.73 us (7%)
  waiting for transfers between devices  3.65 us (6%)
  Pallas kernels  2.3 us (4%)
  other arithmetic  0.99 us (2%)
    all_to_all x4, blocking collectives, gathered(): lax.all_to_all(pay.reshape(count, -1, LANES), axis, 0, 0, tiled=True, axi...  53.1 us
    ppermute x1, starting transfers between devices, body(): down = lax.ppermute(last, 'gy', [(i, i + 1) for i in range(size_y - 1)])  4.73 us
    ppermute x1, waiting for transfers between devices, body(): down = lax.ppermute(last, 'gy', [(i, i + 1) for i in range(size_y - 1)])  3.65 us
  transfers between devices with their start and end apart: 1, of which 1 were waited for; matrix products, arithmetic and copies ran while one was open for 0% of the time, Pallas kernels for 1%

profile of v9, /device:TPU:1, one launch (start us, length us, event | category | flops | bytes accessed | tf_op | source)
XLA Modules:
  0.0 64.9 jit_solution(16190205435641729210)
XLA Ops:
  0.0 1.0 %pad_maximum_fusion.refs_0_.all_ref = f32[512,128]{1,0:T(8,128)S(1)} fusion(f32[256,128]{1,0:T(8,128)} %bitcast.23, f32[256,128]{1,0:T(8,128)} %bitcast.24), kind=kLoop, calls=%fused_computation | loop fusion | flops 65536 | bytes 524288 | tf_op jit(solution)/shard_map/concatenate | solution.py:369
  1.0 0.0 copy-start
  1.0 4.7 %collective-permute-start = (f32[32,128]{1,0:T(8,128)S(1)}, f32[32,128]{1,0:T(8,128)S(1)}, u32[]{:S(2)}, u32[]{:S(2)}) collective-permute-start(f32[32,128]{1,0:T(8,128)S(1)} %shard_map.38), channel_id=1, source_target_pairs={{0,1},{1,2},{2,3},{3,4},{4,5},{5,6},{6,7},{7,8},{8,9},{9,10},{10,1... | collective-permute-start | bytes 49160 | tf_op jit(solution)/shard_map/ppermute | solution.py:371
  5.8 0.0 copy-done
  5.8 0.6 shard_map.37
  6.3 3.6 %collective-permute-done.refs_8_ = f32[32,128]{1,0:T(8,128)S(1)} collective-permute-done((f32[32,128]{1,0:T(8,128)S(1)}, f32[32,128]{1,0:T(8,128)S(1)}, u32[]{:S(2)}, u32[]{:S(2)}) %collective-permute-start) | collective-permute-done | bytes 16416 | tf_op jit(solution)/shard_map/ppermute | solution.py:371
  10.0 0.2 shard_map.39
  10.2 11.2 %all_to_all.20 = f32[8,120,128]{2,1,0:T(8,128)S(1)} all-to-all(f32[8,120,128]{2,1,0:T(8,128)S(1)} %bitcast.20), channel_id=1, replica_groups={{0,16,32,48,64,80,96,112},{128,144,160,176,192,208,224,240},{256,272,28..., dimensions={0} | all-to-all | bytes 983040 | tf_op jit(solution)/shard_map/all_to_all | solution.py:358
  21.4 0.1 shard_map.40
  21.6 19.1 %all_to_all.21 = f32[4,120,128]{2,1,0:T(8,128)S(1)} all-to-all(f32[4,120,128]{2,1,0:T(8,128)S(1)} %bitcast.17), channel_id=1, replica_groups={{0,128,256,384},{16,144,272,400},{32,160,288,416},{48,176,304,432},{64,..., dimensions={0} | all-to-all | bytes 491520 | tf_op jit(solution)/shard_map/all_to_all | solution.py:358
  40.7 0.3 shard_map.41
  41.0 8.5 %all_to_all.22 = f32[4,80,128]{2,1,0:T(8,128)S(1)} all-to-all(f32[4,80,128]{2,1,0:T(8,128)S(1)} %bitcast.21), channel_id=1, replica_groups={{0,1,2,3},{4,5,6,7},{8,9,10,11},{12,13,14,15},{16,17,18,19},{20,21,22,2..., dimensions={0} | all-to-all | bytes 327680 | tf_op jit(solution)/shard_map/all_to_all | solution.py:358
  49.5 14.3 %all_to_all.23 = f32[4,80,128]{2,1,0:T(8,128)S(1)} all-to-all(f32[4,80,128]{2,1,0:T(8,128)S(1)} %bitcast.19), channel_id=1, replica_groups={{0,4,8,12},{1,5,9,13},{2,6,10,14},{3,7,11,15},{16,20,24,28},{17,21,25,2..., dimensions={0} | all-to-all | bytes 327680 | tf_op jit(solution)/shard_map/all_to_all | solution.py:358
  63.8 1.1 %shard_map.43 = f32[256,128]{1,0:T(8,128)} custom-call(f32[320,128]{1,0:T(8,128)S(1)} %bitcast.15, f32[320,128]{1,0:T(8,128)S(1)} %bitcast.18, f32[96,128]{1,0:T(8,128)S(1)} %get-tuple-element.45.refs_12_.refs_2_, f32[16,128]{1,0:T(8,128)S(1)} %get-tuple-element.47.refs_3_, f32[256,128]{1,0:T(8,128)S(1)} %get-tuple-element.29.refs_0_.refs_2_.refs_4_, ...), custom_call_target="tpu_custom_call" | custom-call | tf_op jit(solution)/shard_map/pallas_call | solution.py:397
  (2 shorter events, 0.0 us)
Async XLA Ops:
  1.0 4.8 %copy-start = (f32[16,16,128]{2,1,0:T(8,128)S(1)}, f32[16,16,128]{2,1,0:T(8,128)}, u32[]{:S(2)}) copy-start(f32[16,16,128]{2,1,0:T(8,128)} %param.5) | copy-start | bytes 393220
  1.0 9.0 %collective-permute-start = (f32[32,128]{1,0:T(8,128)S(1)}, f32[32,128]{1,0:T(8,128)S(1)}, u32[]{:S(2)}, u32[]{:S(2)}) collective-permute-start(f32[32,128]{1,0:T(8,128)S(1)} %shard_map.38), channel_id=1, source_target_pairs={{0,1},{1,2},{2,3},{3,4},{4,5},{5,6},{6,7},{7,8},{8,9},{9,10},{10,1... | collective-permute-start | bytes 49160 | tf_op jit(solution)/shard_map/ppermute | solution.py:371
